TPU v7x, 32 devices: a whole 2x2x4 slice. The times are simulated.
32 devices in a mesh: wide: 8 (over z, y), narrow: 4 (over x, core).
Axes of the slice: x: 2, y: 2, z: 4, core: 2. Of those that a mesh axis runs over, the one named last changes fastest.
Arguments:
- adjoint: float32 [3, 512, 256, 256], P(None, 'wide', 'narrow'), may hold values from -6 to 6
- velocity: float32 [3, 512, 256, 256], P(None, 'wide', 'narrow'), may hold values from -6 to 6
- deriv_x: float32 [256, 256], replicated, as said below
- deriv_y: float32 [256, 256], replicated, as said below
- deriv_z: float32 [512, 512], replicated, as said below
- rotor_blocks: int32 [96, 128], replicated, may hold values from 0 to 262143, as said below
- turbine_owner: int32 [96], replicated, may hold values from 0 to 31, as said below
- disk_weight: float32 [96, 128, 128], replicated, may hold values from 0.1 to 1
- thrust: float32 [96], replicated, may hold values from 0.5 to 2
Outputs:
- updated_adjoint: float32 [3, 512, 256, 256], P(None, 'wide', 'narrow')
- turbine_grad: float32 [128, 2], P(('wide', 'narrow'))
Inputs may be any that keep to these rules, and one draw needn't show every extreme that they name: `deriv_x`: entries vanish where the row's block of 64 and the column's block differ by more than one. `deriv_y`: entries vanish where the row's block of 32 and the column's block differ by more than one. `deriv_z`: entries vanish where the row's block of 16 and the column's block differ by more than one. `rotor_blocks`: block id b = (z * 256 + y) * 2 + x block. A rotor's row lists 128 // 2 consecutive z planes times 2 consecutive y lines, all at one x block, z major. `turbine_owner`: devices are numbered wide major over wide and narrow. No device owns more than 4 turbines, and one owns exactly 4.
All inputs are finite; a program needn't handle non-finite values.
Results may differ from a plain program's by a relative error of at most 0.00014.
Values sent between devices are 32-bit elements; how exact they have to be, the bound alone decides.
A program may use at most 256 MiB of HBM per device.

v0:
```python
import math

import jax
import jax.numpy as jnp
from jax import lax
from jax.sharding import PartitionSpec as P

NY = 256


def directional(adjoint, velocity, adj_deriv, vel_deriv, direction):
    advect = velocity[direction][None] * adj_deriv
    stretch = -jnp.sum(adjoint * vel_deriv, axis=0)
    select = (jnp.arange(3) == direction).astype(jnp.float32)[:, None, None, None]
    return advect + select * stretch[None]


def turbine_terms(adjoint, velocity, rotor_blocks, disk_weight, thrust):
    shard_z = adjoint.shape[1]
    shard_y = adjoint.shape[2]
    x_blocks = adjoint.shape[3] // 128
    line_id = rotor_blocks // x_blocks
    block_x = rotor_blocks % x_blocks
    row_y = line_id % NY
    row_z = line_id // NY
    first_z = lax.axis_index("wide") * shard_z
    first_y = lax.axis_index("narrow") * shard_y
    is_local = (
        (row_z >= first_z)
        & (row_z < first_z + shard_z)
        & (row_y >= first_y)
        & (row_y < first_y + shard_y)
    )
    row_index = jnp.where(
        is_local, ((row_z - first_z) * shard_y + row_y - first_y) * x_blocks + block_x, 0
    )
    ax_rows = adjoint[0].reshape(-1, 128)[row_index]
    ay_rows = adjoint[1].reshape(-1, 128)[row_index]
    ux_rows = velocity[0].reshape(-1, 128)[row_index]
    weight = jnp.where(is_local[:, :, None], disk_weight, 0.0)
    thrust_drive = ux_rows * jnp.abs(ux_rows)
    scale = 1.0 / math.sqrt(128.0 * rotor_blocks.shape[1])
    grad_thrust = jnp.sum(weight * ax_rows * thrust_drive, axis=(1, 2)) * scale
    grad_side = jnp.sum(weight * ay_rows * thrust_drive, axis=(1, 2)) * scale
    partial_value = jnp.stack([grad_thrust, grad_side], axis=1)
    weighted = (weight * thrust[:, None, None]).reshape(-1, 128)
    source = jnp.zeros((shard_z * shard_y * x_blocks, 128), jnp.float32)
    source = source.at[row_index.reshape(-1)].add(weighted).reshape(adjoint.shape[1:])
    return (partial_value, source)


def on_device(
    adjoint, velocity, deriv_x, deriv_y, deriv_z, rotor_blocks, turbine_owner, disk_weight, thrust
):
    highest = lax.Precision.HIGHEST
    adj_dx = jnp.einsum("czyk,xk->czyx", adjoint, deriv_x, precision=highest)
    vel_dx = jnp.einsum("czyk,xk->czyx", velocity, deriv_x, precision=highest)
    part_x = directional(adjoint, velocity, adj_dx, vel_dx, 0)
    rows_adj, rows_vel = (
        lax.all_to_all(adjoint, "narrow", split_axis=3, concat_axis=2, tiled=True),
        lax.all_to_all(velocity, "narrow", split_axis=3, concat_axis=2, tiled=True),
    )
    adj_dy = jnp.einsum("czkx,yk->czyx", rows_adj, deriv_y, precision=highest)
    vel_dy = jnp.einsum("czkx,yk->czyx", rows_vel, deriv_y, precision=highest)
    part_y = directional(rows_adj, rows_vel, adj_dy, vel_dy, 1)
    returned_rows = lax.all_to_all(part_y, "narrow", split_axis=2, concat_axis=3, tiled=True)
    cols_adj, cols_vel = (
        lax.all_to_all(adjoint, "wide", split_axis=3, concat_axis=1, tiled=True),
        lax.all_to_all(velocity, "wide", split_axis=3, concat_axis=1, tiled=True),
    )
    col_shape = cols_adj.shape
    flat_adj = cols_adj.reshape(3, col_shape[1], -1)
    flat_vel = cols_vel.reshape(3, col_shape[1], -1)
    adj_dz = jnp.einsum("ckm,zk->czm", flat_adj, deriv_z, precision=highest).reshape(col_shape)
    vel_dz = jnp.einsum("ckm,zk->czm", flat_vel, deriv_z, precision=highest).reshape(col_shape)
    part_z = directional(cols_adj, cols_vel, adj_dz, vel_dz, 2)
    vertical_term = lax.all_to_all(part_z, "wide", split_axis=1, concat_axis=3, tiled=True)
    partial_value, source = turbine_terms(adjoint, velocity, rotor_blocks, disk_weight, thrust)
    forcing = source * jnp.abs(velocity[0]) * adjoint[0]
    select = (jnp.arange(3) == 0).astype(jnp.float32)[:, None, None, None]
    tendency = part_x + returned_rows + vertical_term - select * forcing[None]
    updated = adjoint + 0.2 * tendency
    turbines = turbine_owner.shape[0]
    devices = lax.axis_size("wide") * lax.axis_size("narrow")
    slot_count = (turbines - 2) // devices + 2
    positions = jnp.arange(turbines)
    shared = turbine_owner[:, None] == turbine_owner[None, :]
    earlier = positions[:, None] > positions[None, :]
    slot_rank = jnp.sum((shared & earlier).astype(jnp.int32), axis=1)
    target_slot = turbine_owner * slot_count + slot_rank
    onehot = (jnp.arange(devices * slot_count)[:, None] == target_slot[None, :]).astype(jnp.float32)
    owner_term = jnp.dot(
        onehot, partial_value, precision=highest, preferred_element_type=jnp.float32
    )
    owner_share = lax.psum_scatter(owner_term, ("wide", "narrow"), scatter_dimension=0, tiled=True)
    return (updated, owner_share)


def solution(mesh):
    return jax.shard_map(
        on_device,
        mesh=mesh,
        in_specs=(
            P(None, "wide", "narrow", None),
            P(None, "wide", "narrow", None),
            P(),
            P(),
            P(),
            P(),
            P(),
            P(),
            P(),
        ),
        out_specs=(P(None, "wide", "narrow", None), P(("wide", "narrow"), None)),
        check_vma=False,
    )
```

profile of v0, /device:TPU:0, one launch (start us, length us, event | category | flops | bytes accessed | tf_op | source)
XLA Modules:
  0.0 2092.6 jit_solution(13394573074821689449)
XLA Ops:
  24.2 33.3 %reshape.171 = f32[4,1,786432]{2,1,0:T(1,128)} reshape(f32[256,3,64,64]{3,2,1,0:T(8,128)} %bitcast.125) | data formatting | bytes 25165824
  87.3 33.5 %reshape.173 = f32[4,1,786432]{2,1,0:T(1,128)} reshape(f32[256,3,64,64]{3,2,1,0:T(8,128)} %bitcast.127) | data formatting | bytes 25165824
  120.7 81.8 %all-to-all-done.1 = f32[4,1,786432]{2,1,0:T(1,128)} async-done(((f32[4,1,786432]{2,1,0:T(1,128)}), f32[4,1,786432]{2,1,0:T(1,128)}, u32[]{:S(2)}, u32[]{:S(2)}) %all-to-all-start.1) | async-done | bytes 12582944 | tf_op jit(solution)/shard_map/all_to_all | solution.py:60
  229.3 117.6 %all-to-all-done = f32[4,1,786432]{2,1,0:T(1,128)} async-done(((f32[4,1,786432]{2,1,0:T(1,128)}), f32[4,1,786432]{2,1,0:T(1,128)}, u32[]{:S(2)}, u32[]{:S(2)}) %all-to-all-start) | async-done | bytes 12582944 | tf_op jit(solution)/shard_map/all_to_all | solution.py:61
  374.6 252.4 %all-to-all-done.3 = f32[8,1,393216]{2,1,0:T(1,128)} async-done(((f32[8,1,393216]{2,1,0:T(1,128)}), f32[8,1,393216]{2,1,0:T(1,128)}, u32[]{:S(2)}, u32[]{:S(2)}) %all-to-all-start.3) | async-done | bytes 12582944 | tf_op jit(solution)/shard_map/all_to_all | solution.py:69
  632.9 39.6 %reduce.5 = f32[4,786432]{1,0:T(4,128)} reduce(f32[4,1,786432]{2,1,0:T(1,128)} %all-to-all-done, f32[]{:T(128)} %broadcast.137), dimensions={1}, to_apply=%all_to_all.74.reduce_sub_computation | reduce | bytes 25165828 | tf_op jit(solution)/shard_map/all_to_all | solution.py:61
  672.5 31.9 %reshape.174 = f32[256,3,64,64]{3,2,1,0:T(8,128)} reshape(f32[4,786432]{1,0:T(4,128)} %reduce.5) | data formatting | bytes 25165824
  704.4 30.3 %copy.151 = f32[3,64,64,4,64]{2,3,4,1,0:T(4,128)} copy(f32[3,64,64,4,64]{2,1,0,4,3:T(8,128)} %bitcast.135) | data formatting | bytes 25165824 | tf_op jit(solution)/shard_map/all_to_all | solution.py:61
  765.5 39.9 %reduce.4 = f32[4,786432]{1,0:T(4,128)} reduce(f32[4,1,786432]{2,1,0:T(1,128)} %all-to-all-done.1, f32[]{:T(128)} %broadcast.137), dimensions={1}, to_apply=%all_to_all.77.reduce_sub_computation | reduce | bytes 25165828 | tf_op jit(solution)/shard_map/all_to_all | solution.py:60
  805.4 32.1 %reshape.172 = f32[256,3,64,64]{3,2,1,0:T(8,128)} reshape(f32[4,786432]{1,0:T(4,128)} %reduce.4) | data formatting | bytes 25165824
  837.5 30.2 %copy.150 = f32[3,64,64,4,64]{2,3,4,1,0:T(4,128)} copy(f32[3,64,64,4,64]{2,1,0,4,3:T(8,128)} %bitcast.136) | data formatting | bytes 25165824 | tf_op jit(solution)/shard_map/all_to_all | solution.py:60
  958.1 33.3 %reshape.175 = f32[4,1,786432]{2,1,0:T(1,128)} reshape(f32[256,3,64,64]{3,2,1,0:T(8,128)} %bitcast.138) | data formatting | bytes 25165824
  998.7 36.9 %reduce.2 = f32[8,393216]{1,0:T(8,128)} reduce(f32[8,1,393216]{2,1,0:T(1,128)} %all-to-all-done.3, f32[]{:T(128)} %broadcast.137), dimensions={1}, to_apply=%all_to_all.86.reduce_sub_computation | reduce | bytes 25165828 | tf_op jit(solution)/shard_map/all_to_all | solution.py:69
  1058.2 25.0 %copy.120 = f32[3,64,64,256]{2,3,1,0:T(8,128)} copy(f32[3,64,64,256]{2,1,0,3:T(8,128)} %bitcast.131) | data formatting | bytes 25165824 | tf_op jit(solution)/shard_map/all_to_all | solution.py:69
  1083.2 25.9 %copy.127 = f32[3,8,64,64,32]{2,1,4,3,0:T(8,128)} copy(f32[3,8,64,64,32]{3,2,0,4,1:T(8,128)} %bitcast.132) | data formatting | bytes 25165824 | tf_op jit(solution)/shard_map/all_to_all | solution.py:69
  1130.0 24.5 %convolution_bitcast_fusion = f32[3,512,2048]{2,1,0:T(8,128)} fusion(f32[3,512,2048]{1,2,0:T(8,128)} %reshape.115, f32[512,512]{1,0:T(8,128)S(1)} %copy-done), kind=kOutput, calls=%fused_computation.19 | convolution fusion | flops 19327352832 | bytes 26214400 | tf_op jit(solution)/shard_map/ckm,zk->czm/dot_general | solution.py:75
  1185.9 28.5 %copy.130 = f32[3,8,64,64,32]{3,4,1,2,0:T(8,128)} copy(f32[3,8,64,64,32]{2,1,4,3,0:T(8,128)} %reshape.116) | data formatting | bytes 25165824 | tf_op jit(solution)/shard_map/reshape | solution.py:75
  1214.4 36.9 %reduce.1 = f32[8,393216]{1,0:T(8,128)} reduce(f32[8,1,393216]{2,1,0:T(1,128)} %all-to-all-done.4, f32[]{:T(128)} %broadcast.137), dimensions={1}, to_apply=%all_to_all.89.reduce_sub_computation | reduce | bytes 25165828 | tf_op jit(solution)/shard_map/all_to_all | solution.py:68
  1273.9 25.3 %copy.123 = f32[3,64,64,256]{2,3,1,0:T(8,128)} copy(f32[3,64,64,256]{2,1,0,3:T(8,128)} %bitcast.129) | data formatting | bytes 25165824 | tf_op jit(solution)/shard_map/all_to_all | solution.py:68
  1340.4 25.9 %copy.124 = f32[3,8,64,64,32]{2,1,4,3,0:T(8,128)} copy(f32[3,8,64,64,32]{3,2,0,4,1:T(8,128)} %bitcast.130) | data formatting | bytes 25165824 | tf_op jit(solution)/shard_map/all_to_all | solution.py:68
  1387.2 24.7 %convolution_bitcast_fusion.1 = f32[3,512,2048]{2,1,0:T(8,128)} fusion(f32[3,512,2048]{1,2,0:T(8,128)} %reshape.113, f32[512,512]{1,0:T(8,128)S(1)} %copy-done), kind=kOutput, calls=%fused_computation.20 | convolution fusion | flops 19327352832 | bytes 26214400 | tf_op jit(solution)/shard_map/ckm,zk->czm/dot_general | solution.py:74
  1465.2 23.6 %copy.132 = f32[3,512,64,32]{2,3,0,1:T(8,128)} copy(f32[3,512,64,32]{1,3,2,0:T(8,128)} %multiply_add_fusion.1) | data formatting | bytes 25165824 | tf_op jit(solution)/shard_map/add | solution.py:15
  1524.4 87.3 %scatter_custom_fusion = f32[8192,128]{1,0:T(8,128)} fusion(s32[12288]{0:T(1024)S(1)} %bitcast.152, f32[12288,128]{1,0:T(8,128)} %bitcast.150, f32[]{:T(128)} %constant.62.clone.1), kind=kCustom, calls=%fused_computation.22 | custom fusion | flops 1572864 | bytes 4194816 | tf_op jit(solution)/shard_map/scatter-add | solution.py:48
  1639.5 43.2 %gather_fusion = f32[12288,128]{1,0:T(8,128)} fusion(f32[8192,128]{1,0:T(8,128)} %reshape_squeeze.9, s32[12288]{0:T(1024)S(1)} %get-tuple-element.4), kind=kCustom, calls=%fused_computation | custom fusion | bytes 12632064 | tf_op jit(solution)/shard_map/gather | solution.py:37
  1682.8 43.2 %gather_fusion.1 = f32[12288,128]{1,0:T(8,128)} fusion(f32[8192,128]{1,0:T(8,128)} %reshape_squeeze.10, s32[12288]{0:T(1024)S(1)} %get-tuple-element.4), kind=kCustom, calls=%fused_computation.1 | custom fusion | bytes 12632064 | tf_op jit(solution)/shard_map/gather | solution.py:39
  1730.8 43.2 %gather_fusion.2 = f32[12288,128]{1,0:T(8,128)} fusion(f32[8192,128]{1,0:T(8,128)} %reshape_squeeze.11, s32[12288]{0:T(1024)S(1)} %get-tuple-element.4), kind=kCustom, calls=%fused_computation.2 | custom fusion | bytes 12632064 | tf_op jit(solution)/shard_map/gather | solution.py:38
  1802.5 40.9 %all-reduce = f32[128,2]{0,1:T(2,128)S(1)} all-reduce(f32[128,2]{0,1:T(2,128)S(1)} %fusion.10), channel_id=2, replica_groups=mesh['wide'=8,'narrow'=4] {'wide','narrow'}, use_global_device_ids=true, to_apply=%region_7.8.clone | all-reduce | flops 256 | bytes 2048
  1844.0 39.8 %reduce.6 = f32[4,786432]{1,0:T(4,128)} reduce(f32[4,1,786432]{2,1,0:T(1,128)} %all-to-all-done.2, f32[]{:T(128)} %broadcast.137), dimensions={1}, to_apply=%all_to_all.82.reduce_sub_computation | reduce | bytes 25165828 | tf_op jit(solution)/shard_map/all_to_all | solution.py:66
  1883.8 31.9 %reshape.176 = f32[256,3,64,64]{3,2,1,0:T(8,128)} reshape(f32[4,786432]{1,0:T(4,128)} %reduce.6) | data formatting | bytes 25165824
  1915.7 30.2 %copy.149 = f32[3,64,4,64,64]{4,2,3,1,0:T(4,128)} copy(f32[3,64,4,64,64]{4,1,0,3,2:T(8,128)} %bitcast.141) | data formatting | bytes 25165824 | tf_op jit(solution)/shard_map/all_to_all | solution.py:66
  1969.2 37.3 %reduce.3 = f32[8,393216]{1,0:T(8,128)} reduce(f32[8,1,393216]{2,1,0:T(1,128)} %all-to-all-done.5, f32[]{:T(128)} %broadcast.137), dimensions={1}, to_apply=%all_to_all.92.reduce_sub_computation | reduce | bytes 25165828 | tf_op jit(solution)/shard_map/all_to_all | solution.py:77
  2065.5 26.9 %multiply_add_fusion = f32[3,64,64,256]{3,2,1,0:T(8,128)} fusion(f32[3,64,64,256]{3,2,1,0:T(8,128)} %param.9, f32[3,64,64,256]{3,2,1,0:T(8,128)} %copy.135, f32[3,64,64,256]{3,2,1,0:T(8,128)} %all_to_all.85, f32[64,64,256]{2,1,0:T(8,128)} %get-tuple-element.8, f32[64,64,256]{2,1,0:T(8,128)} %neg.24, f32[3]{0:T(128)S(1)} %compare_convert_fusion.2, ...), kind=kOutput, calls=%fused_computation.12 | convolution fusion | flops 9691987968 | bytes 63176716 | tf_op jit(solution)/shard_map/czyk,xk->czyx/dot_general | solution.py:56
  (75 shorter events, 634.5 us)
Async XLA Ops:
  0.6 1129.4 %copy-start = (f32[512,512]{1,0:T(8,128)S(1)}, f32[512,512]{1,0:T(8,128)}, u32[]{:S(2)}) copy-start(f32[512,512]{1,0:T(8,128)} %param.13) | copy-start | bytes 3145732
  57.5 145.0 %all-to-all-start.1 = ((f32[4,1,786432]{2,1,0:T(1,128)}), f32[4,1,786432]{2,1,0:T(1,128)}, u32[]{:S(2)}, u32[]{:S(2)}) async-start(f32[4,1,786432]{2,1,0:T(1,128)} %reshape.171), calls=%async_computation.1 | async-start | bytes 25165824 | tf_op jit(solution)/shard_map/all_to_all | solution.py:60
  202.5 144.4 %all-to-all-start = ((f32[4,1,786432]{2,1,0:T(1,128)}), f32[4,1,786432]{2,1,0:T(1,128)}, u32[]{:S(2)}, u32[]{:S(2)}) async-start(f32[4,1,786432]{2,1,0:T(1,128)} %reshape.173), calls=%async_computation | async-start | bytes 25165824 | tf_op jit(solution)/shard_map/all_to_all | solution.py:61
  346.9 280.0 %all-to-all-start.3 = ((f32[8,1,393216]{2,1,0:T(1,128)}), f32[8,1,393216]{2,1,0:T(1,128)}, u32[]{:S(2)}, u32[]{:S(2)}) async-start(f32[8,1,393216]{2,1,0:T(1,128)} %reshape.167), calls=%async_computation.3 | async-start | bytes 25165824 | tf_op jit(solution)/shard_map/all_to_all | solution.py:69
  627.0 364.5 %all-to-all-start.4 = ((f32[8,1,393216]{2,1,0:T(1,128)}), f32[8,1,393216]{2,1,0:T(1,128)}, u32[]{:S(2)}, u32[]{:S(2)}) async-start(f32[8,1,393216]{2,1,0:T(1,128)} %reshape.165), calls=%async_computation.4 | async-start | bytes 25165824 | tf_op jit(solution)/shard_map/all_to_all | solution.py:68
  867.7 23.2 %copy-start.1 = (f32[256,256]{1,0:T(8,128)S(1)}, f32[256,256]{1,0:T(8,128)}, u32[]{:S(2)}) copy-start(f32[256,256]{1,0:T(8,128)} %param.12) | copy-start | bytes 786436
  991.5 517.8 %all-to-all-start.2 = ((f32[4,1,786432]{2,1,0:T(1,128)}), f32[4,1,786432]{2,1,0:T(1,128)}, u32[]{:S(2)}, u32[]{:S(2)}) async-start(f32[4,1,786432]{2,1,0:T(1,128)} %reshape.175), calls=%async_computation.2 | async-start | bytes 25165824 | tf_op jit(solution)/shard_map/all_to_all | solution.py:66
  1432.9 18.4 copy-start.4
  1509.2 6.1 copy-start.3
  1509.2 6.2 copy-start.5
  1509.2 459.9 %all-to-all-start.5 = ((f32[8,1,393216]{2,1,0:T(1,128)}), f32[8,1,393216]{2,1,0:T(1,128)}, u32[]{:S(2)}, u32[]{:S(2)}) async-start(f32[8,1,393216]{2,1,0:T(1,128)} %reshape.169), calls=%async_computation.5 | async-start | bytes 25165824 | tf_op jit(solution)/shard_map/all_to_all | solution.py:77
  1730.8 43.2 %copy-start.2 = (f32[256,256]{1,0:T(8,128)S(1)}, f32[256,256]{1,0:T(8,128)}, u32[]{:S(2)}) copy-start(f32[256,256]{1,0:T(8,128)} %param.11) | copy-start | bytes 786436
  1774.0 17.8 copy-start.6
where the time goes:
time: 2110 us; the launch traced here: 2090 us
  local copies, waits for them, and re-layouts  1040 us (49%)
  waiting for transfers between devices  452 us (21%)
  other arithmetic  392 us (19%)
  matrix products  125 us (6%)
  blocking collectives  40.9 us (2%)
  starting transfers between devices  37.9 us (2%)
    unnamed x29, local copies, waits for them, and re-layouts  373 us
    all_to_all x1, waiting for transfers between devices, on_device(): lax.all_to_all(velocity, 'wide', split_axis=3, concat_axis=1, tiled=True)  252 us
    all_to_all x1, waiting for transfers between devices, on_device(): lax.all_to_all(velocity, 'narrow', split_axis=3, concat_axis=2, tiled=True)  118 us
    scatter-add x1, other arithmetic, turbine_terms(): source.at[row_index.reshape(-1)].add(weighted).reshape(adjoint.shape[1:])  87.3 us
    all_to_all x1, waiting for transfers between devices, on_device(): lax.all_to_all(adjoint, 'narrow', split_axis=3, concat_axis=2, tiled=True)  81.8 us
    all_to_all x2, local copies, waits for them, and re-layouts, on_device(): lax.all_to_all(velocity, 'narrow', split_axis=3, concat_axis=2, tiled=True)  53.4 us
    all_to_all x2, local copies, waits for them, and re-layouts, on_device(): lax.all_to_all(adjoint, 'narrow', split_axis=3, concat_axis=2, tiled=True)  53.4 us
    all_to_all x2, local copies, waits for them, and re-layouts, on_device(): lax.all_to_all(part_y, 'narrow', split_axis=2, concat_axis=3, tiled=True)  53.4 us
  transfers between devices with their start and end apart: 6, of which 3 were waited for; matrix products, arithmetic and copies ran while one was open for 63% of the time, Pallas kernels for 0%

commit v1 on v0

v1 whole, which is shorter than its diff:
```python
import functools
import math

import jax
import jax.numpy as jnp
from jax import lax
from jax.experimental import pallas as pl
from jax.experimental.pallas import tpu as pltpu
from jax.sharding import PartitionSpec as P

NY = 256
BY = 32
BAND = 16
RY = 2
STEP = 0.2
GROUP = 8
VMEM = 56 * 1024 * 1024


def params():
    return pltpu.CompilerParams(vmem_limit_bytes=VMEM)


def cost(flops, moved):
    return pl.CostEstimate(flops=int(flops), bytes_accessed=int(moved), transcendentals=0)


def split(value):
    high = value.astype(jnp.bfloat16)
    low = (value - high.astype(jnp.float32)).astype(jnp.bfloat16)
    return high, low


def dot(left, right):
    return jnp.dot(left, right, preferred_element_type=jnp.float32)


def split_matrix(matrix):
    high = lax.reduce_precision(matrix, 8, 7)
    return high, matrix - high


def stacked(matrix):
    high, low = split_matrix(matrix)
    top = jnp.concatenate([high, high], axis=1)
    bottom = jnp.concatenate([low, jnp.zeros_like(low)], axis=1)
    return jnp.concatenate([top, bottom], axis=0).astype(jnp.bfloat16)


def paired(matrix, axis):
    high, low = split_matrix(matrix)
    return jnp.concatenate([high, low], axis=axis).astype(jnp.bfloat16)


def apply_stacked(matrix, values):
    product = dot(matrix, jnp.concatenate(split(values), axis=0))
    rows = product.shape[0] // 2
    return product[:rows] + product[rows:]


def turbine_kernel(
    count, shard, zs, ys, xs, thrust, a0, a1, u0, weight, source, grad0, grad1
):
    shard_z, shard_y, planes = shard
    step = pl.program_id(0)

    @pl.when(step == 0)
    def _():
        source[...] = jnp.zeros_like(source)

    grad0[...] = jnp.zeros_like(grad0)
    grad1[...] = jnp.zeros_like(grad1)
    for slot in range(count):
        turbine = step * count + slot
        first_z = zs[turbine]
        low = jnp.maximum(first_z, 0)
        high = jnp.minimum(first_z + planes, shard_z)
        lanes = pl.ds(pl.multiple_of(xs[turbine] * 128, 128), 128)
        for line in range(RY):
            y = ys[turbine] + line

            @pl.when((y >= 0) & (y < shard_y) & (high > low))
            def _():
                tile = pl.ds(pl.multiple_of(y // 8 * 8, 8), 8)
                chosen = lax.broadcasted_iota(jnp.int32, (8, 128), 0) == y % 8

                def body(z, sums):
                    row = weight[slot, pl.ds((z - first_z) * RY + line, 1), :]
                    row = jnp.where(chosen, jnp.broadcast_to(row, (8, 128)), 0.0)
                    at = (z, tile, lanes)
                    u = u0[at]
                    driven = row * u * jnp.abs(u)
                    source[at] += row * thrust[turbine]
                    return sums[0] + driven * a0[at], sums[1] + driven * a1[at]

                zero = jnp.zeros((8, 128), jnp.float32)
                sums = lax.fori_loop(low, high, body, (zero, zero))
                grad0[slot : slot + 1, :] += jnp.sum(sums[0], axis=0, keepdims=True)
                grad1[slot : slot + 1, :] += jnp.sum(sums[1], axis=0, keepdims=True)


def turbine_terms(adjoint, velocity, rotor_blocks, disk_weight, thrust):
    _, shard_z, shard_y, extent = adjoint.shape
    x_blocks = extent // 128
    turbines, blocks = rotor_blocks.shape
    count = 8
    first = rotor_blocks[:, 0]
    line = first // x_blocks
    zs = line // NY - lax.axis_index("wide") * shard_z
    ys = line % NY - lax.axis_index("narrow") * shard_y
    xs = first % x_blocks
    field = lambda c: pl.BlockSpec((None, shard_z, shard_y, extent), lambda i, *_: (c, 0, 0, 0))
    sums = pl.BlockSpec((count, 128), lambda i, *_: (i, 0))
    return pl.pallas_call(
        functools.partial(turbine_kernel, count, (shard_z, shard_y, blocks // RY)),
        grid_spec=pltpu.PrefetchScalarGridSpec(
            num_scalar_prefetch=4,
            grid=(turbines // count,),
            in_specs=[
                field(0),
                field(1),
                field(0),
                pl.BlockSpec((count, blocks, 128), lambda i, *_: (i, 0, 0)),
            ],
            out_specs=[
                pl.BlockSpec((shard_z, shard_y, extent), lambda i, *_: (0, 0, 0)),
                sums,
                sums,
            ],
        ),
        out_shape=[
            jax.ShapeDtypeStruct((shard_z, shard_y, extent), jnp.float32),
            jax.ShapeDtypeStruct((turbines, 128), jnp.float32),
            jax.ShapeDtypeStruct((turbines, 128), jnp.float32),
        ],
        compiler_params=params(),
        cost_estimate=cost(1e6, 3e7),
        name="turbine_terms",
    )(zs, ys, xs, thrust, adjoint, adjoint, velocity, disk_weight)


def z_local_kernel(matrix, adjoint, velocity, out):
    _, shard_z, group, extent = adjoint.shape
    rows = shard_z * group
    both = matrix[...]
    high_part = both[:rows]

    def derivative(values):
        high, low = split(values.reshape(rows, extent))
        wide = dot(both, high)
        total = wide[:rows] + wide[rows:] + dot(high_part, low)
        return total.reshape(shard_z, group, extent)

    carrier = velocity[2]
    stretch = adjoint[0] * derivative(velocity[0])
    stretch += adjoint[1] * derivative(velocity[1])
    stretch += adjoint[2] * derivative(velocity[2])
    out[0] = carrier * derivative(adjoint[0])
    out[1] = carrier * derivative(adjoint[1])
    out[2] = carrier * derivative(adjoint[2]) - stretch


def z_local(matrix, adjoint, velocity):
    _, shard_z, shard_y, extent = adjoint.shape
    block = pl.BlockSpec((3, shard_z, GROUP, extent), lambda i: (0, 0, i, 0))
    return pl.pallas_call(
        z_local_kernel,
        grid=(shard_y // GROUP,),
        in_specs=[pl.BlockSpec(matrix.shape, lambda i: (0, 0)), block, block],
        out_specs=block,
        out_shape=jax.ShapeDtypeStruct(adjoint.shape, jnp.float32),
        compiler_params=params(),
        cost_estimate=cost(2e10, 4e7),
        name="z_local",
    )(matrix, adjoint, velocity)


def xy_kernel(
    matrix_x, matrix_ya, matrix_yv, edge_low, edge_high,
    adjoint, velocity, halo_low, halo_high, source, tendency, out, back_low, back_high,
):
    _, planes, shard_y, extent = adjoint.shape
    rows = planes * shard_y
    x_high = matrix_x[:, :extent]
    x_low = matrix_x[:, extent:]

    def along_x(values):
        high, low = split(values.reshape(rows, extent))
        total = dot(high, x_high) + (dot(low, x_high) + dot(high, x_low))
        return total.reshape(planes, shard_y, extent)

    a0, a1, a2 = adjoint[0], adjoint[1], adjoint[2]
    u = velocity[0]
    stretch = a0 * along_x(velocity[0])
    stretch += a1 * along_x(velocity[1])
    stretch += a2 * along_x(velocity[2])
    out[0] = tendency[0] + u * along_x(a0) - stretch - source[...] * jnp.abs(u) * a0
    out[1] = tendency[1] + u * along_x(a1)
    out[2] = tendency[2] + u * along_x(a2)
    for plane in range(planes):
        stretch = jnp.zeros((shard_y, extent), jnp.float32)
        low_sum = jnp.zeros((BY, extent), jnp.float32)
        high_sum = jnp.zeros((BY, extent), jnp.float32)
        carrier = velocity[1, plane]
        for c in range(3):
            value = velocity[c, plane]
            here = adjoint[c, plane]
            below = halo_low[c, plane]
            above = halo_high[c, plane]
            stretch += here * apply_stacked(matrix_yv[...], value)
            low_sum += below * apply_stacked(edge_low[...], value[:BY])
            high_sum += above * apply_stacked(edge_high[...], value[shard_y - BY :])
            column = jnp.concatenate([below, here, above], axis=0)
            out[c, plane] += carrier * apply_stacked(matrix_ya[...], column)
        out[1, plane] -= stretch
        back_low[plane] = low_sum
        back_high[plane] = high_sum


def xy_terms(matrices, adjoint, velocity, halo_low, halo_high, source, tendency):
    _, shard_z, shard_y, extent = adjoint.shape
    planes = 4
    whole = lambda m: pl.BlockSpec(m.shape, lambda i: (0, 0))
    block = pl.BlockSpec((3, planes, shard_y, extent), lambda i: (0, i, 0, 0))
    halo = pl.BlockSpec((3, planes, BY, extent), lambda i: (0, i, 0, 0))
    back = pl.BlockSpec((planes, BY, extent), lambda i: (i, 0, 0))
    plane = pl.BlockSpec((planes, shard_y, extent), lambda i: (i, 0, 0))
    back_shape = jax.ShapeDtypeStruct((shard_z, BY, extent), jnp.float32)
    return pl.pallas_call(
        xy_kernel,
        grid=(shard_z // planes,),
        in_specs=[whole(m) for m in matrices] + [block, block, halo, halo, plane, block],
        out_specs=[block, back, back],
        out_shape=[jax.ShapeDtypeStruct(adjoint.shape, jnp.float32), back_shape, back_shape],
        compiler_params=params(),
        cost_estimate=cost(2e10, 7e7),
        name="xy_terms",
    )(*matrices, adjoint, velocity, halo_low, halo_high, source, tendency)


def z_back_kernel(edge_low, edge_high, vel_low, vel_high, halo_low, halo_high, back_low, back_high):
    _, band, group, extent = vel_low.shape
    rows = band * group
    for edge, vel, halo, back in (
        (edge_low, vel_low, halo_low, back_low),
        (edge_high, vel_high, halo_high, back_high),
    ):
        total = jnp.zeros((rows, extent), jnp.float32)
        for c in range(3):
            value = vel[c].reshape(rows, extent)
            total += halo[c].reshape(rows, extent) * apply_stacked(edge[...], value)
        back[...] = total.reshape(band, group, extent)


def z_back(edge_low, edge_high, velocity, halo_low, halo_high):
    _, shard_z, shard_y, extent = velocity.shape
    last = shard_z // BAND - 1
    whole = lambda m: pl.BlockSpec(m.shape, lambda i: (0, 0))
    edge = lambda at: pl.BlockSpec((3, BAND, GROUP, extent), lambda i: (0, at, i, 0))
    back = pl.BlockSpec((BAND, GROUP, extent), lambda i: (0, i, 0))
    shape = jax.ShapeDtypeStruct((BAND, shard_y, extent), jnp.float32)
    return pl.pallas_call(
        z_back_kernel,
        grid=(shard_y // GROUP,),
        in_specs=[whole(edge_low), whole(edge_high), edge(0), edge(last), edge(0), edge(0)],
        out_specs=[back, back],
        out_shape=[shape, shape],
        compiler_params=params(),
        cost_estimate=cost(3e9, 2e7),
        name="z_back",
    )(edge_low, edge_high, velocity, velocity, halo_low, halo_high)


def combine_kernel(
    from_low, from_high, adjoint, carrier, tendency, halo_low, halo_high, stretch_y, out
):
    _, shard_z, group, extent = adjoint.shape
    rows = BAND * group
    top = shard_z - BAND
    for c in range(3):
        total = tendency[c]
        if c == 1:
            total = total - stretch_y[...]
        out[c] = adjoint[c] + STEP * total
        for matrix, halo, at in ((from_low, halo_low, 0), (from_high, halo_high, top)):
            part = apply_stacked(matrix[...], halo[c].reshape(rows, extent))
            planes = slice(at, at + BAND)
            out[c, planes] += STEP * (carrier[planes] * part.reshape(BAND, group, extent))


def combine(from_low, from_high, adjoint, velocity, tendency, halo_low, halo_high, stretch_y):
    _, shard_z, shard_y, extent = adjoint.shape
    whole = lambda m: pl.BlockSpec(m.shape, lambda i: (0, 0))
    block = pl.BlockSpec((3, shard_z, GROUP, extent), lambda i: (0, 0, i, 0))
    carrier = pl.BlockSpec((None, shard_z, GROUP, extent), lambda i: (2, 0, i, 0))
    halo = pl.BlockSpec((3, BAND, GROUP, extent), lambda i: (0, 0, i, 0))
    plane = pl.BlockSpec((shard_z, GROUP, extent), lambda i: (0, i, 0))
    return pl.pallas_call(
        combine_kernel,
        grid=(shard_y // GROUP,),
        in_specs=[whole(from_low), whole(from_high), block, carrier, block, halo, halo, plane],
        out_specs=block,
        out_shape=jax.ShapeDtypeStruct(adjoint.shape, jnp.float32),
        compiler_params=params(),
        cost_estimate=cost(3e9, 5e7),
        name="combine",
    )(from_low, from_high, adjoint, velocity, tendency, halo_low, halo_high, stretch_y)


def finish_kernel(back_low, back_high, updated, out):
    back = jnp.where(pl.program_id(0) == 0, back_low[...], back_high[...])
    out[...] = updated[...] - STEP * back


def finish(updated, back_low, back_high):
    _, shard_z, shard_y, extent = updated.shape
    last = shard_z // BAND - 1
    lines = 16
    edge = pl.BlockSpec((None, BAND, lines, extent), lambda i, j: (2, i * last, j, 0))
    back = pl.BlockSpec((BAND, lines, extent), lambda i, j: (0, j, 0))
    return pl.pallas_call(
        finish_kernel,
        grid=(2, shard_y // lines),
        in_specs=[back, back, edge],
        out_specs=edge,
        out_shape=jax.ShapeDtypeStruct(updated.shape, jnp.float32),
        input_output_aliases={2: 0},
        compiler_params=params(),
        cost_estimate=cost(1e6, 6e6),
        name="finish",
    )(back_low, back_high, updated)


def send_up(value, axis):
    size = lax.axis_size(axis)
    return lax.ppermute(value, axis, [(i, i + 1) for i in range(size - 1)])


def send_down(value, axis):
    size = lax.axis_size(axis)
    return lax.ppermute(value, axis, [(i + 1, i) for i in range(size - 1)])


def windows(matrix, first, shard, halo):
    padded = jnp.pad(matrix, halo)
    rows = lax.dynamic_slice(padded, (first + halo, first), (shard, shard + 2 * halo))
    to_low = lax.dynamic_slice(padded, (first, first + halo), (halo, halo))
    to_high = lax.dynamic_slice(padded, (first + shard + halo, first + shard), (halo, halo))
    return rows, to_low, to_high


def owner_rows(partial_value, turbine_owner):
    turbines = turbine_owner.shape[0]
    devices = lax.axis_size("wide") * lax.axis_size("narrow")
    slot_count = (turbines - 2) // devices + 2
    device = lax.axis_index("wide") * lax.axis_size("narrow") + lax.axis_index("narrow")
    gathered = lax.all_gather(partial_value, ("wide", "narrow"), axis=0, tiled=False)
    grad = jnp.sum(gathered, axis=0)
    positions = jnp.arange(turbines)
    shared = turbine_owner[:, None] == turbine_owner[None, :]
    earlier = positions[:, None] > positions[None, :]
    slot_rank = jnp.sum((shared & earlier).astype(jnp.int32), axis=1)
    mine = (turbine_owner[None, :] == device) & (jnp.arange(slot_count)[:, None] == slot_rank[None, :])
    return jnp.sum(jnp.where(mine[:, None, :], grad[None], 0.0), axis=2)


def on_device(
    adjoint, velocity, deriv_x, deriv_y, deriv_z, rotor_blocks, turbine_owner, disk_weight, thrust
):
    _, shard_z, shard_y, extent = adjoint.shape
    z_low = send_up(adjoint[:, shard_z - BAND :], "wide")
    z_high = send_down(adjoint[:, :BAND], "wide")
    y_low = send_up(adjoint[:, :, shard_y - BY :], "narrow")
    y_high = send_down(adjoint[:, :, :BY], "narrow")

    rows_z, z_to_low, z_to_high = windows(
        deriv_z, lax.axis_index("wide") * shard_z, shard_z, BAND
    )
    rows_y, y_to_low, y_to_high = windows(
        deriv_y, lax.axis_index("narrow") * shard_y, shard_y, BY
    )
    lanes = jnp.eye(GROUP, dtype=jnp.float32)
    spread = lambda m: jnp.kron(m, lanes)

    source, grad0, grad1 = turbine_terms(adjoint, velocity, rotor_blocks, disk_weight, thrust)
    scale = 1.0 / math.sqrt(128.0 * rotor_blocks.shape[1])
    partial_value = jnp.stack([jnp.sum(grad0, axis=1), jnp.sum(grad1, axis=1)]) * scale
    turbine_grad = owner_rows(partial_value, turbine_owner)

    local_z = paired(spread(rows_z[:, BAND : BAND + shard_z]), 0)
    tendency = z_local(local_z, adjoint, velocity)
    matrices = (
        paired(deriv_x.T, 1),
        stacked(rows_y),
        stacked(rows_y[:, BY : BY + shard_y]),
        stacked(y_to_low),
        stacked(y_to_high),
    )
    tendency, y_back_low, y_back_high = xy_terms(
        matrices, adjoint, velocity, y_low, y_high, source, tendency
    )
    stretch_low = send_up(y_back_high, "narrow")
    stretch_high = send_down(y_back_low, "narrow")
    rest = shard_y - BY
    stretch_y = jnp.pad(stretch_low, ((0, 0), (0, rest), (0, 0))) + jnp.pad(
        stretch_high, ((0, 0), (rest, 0), (0, 0))
    )
    z_back_low, z_back_high = z_back(
        stacked(spread(z_to_low)), stacked(spread(z_to_high)), velocity, z_low, z_high
    )
    last_low = send_up(z_back_high, "wide")
    last_high = send_down(z_back_low, "wide")
    updated = combine(
        stacked(spread(rows_z[:BAND, :BAND])),
        stacked(spread(rows_z[shard_z - BAND :, BAND + shard_z :])),
        adjoint, velocity, tendency, z_low, z_high, stretch_y,
    )
    return finish(updated, last_low, last_high), turbine_grad


def solution(mesh):
    return jax.shard_map(
        on_device,
        mesh=mesh,
        in_specs=(
            P(None, "wide", "narrow", None),
            P(None, "wide", "narrow", None),
            P(),
            P(),
            P(),
            P(),
            P(),
            P(),
            P(),
        ),
        out_specs=(P(None, "wide", "narrow", None), P(("wide", "narrow"), None)),
        check_vma=False,
    )
```

time: 2110 us -> 266 us (0.13)
  local copies, waits for them, and re-layouts: 1040 us -> 44.8 us
  waiting for transfers between devices: 452 us -> 22.8 us
  other arithmetic: 392 us -> 25.4 us
  matrix products: 125 us -> 0 us
  Pallas kernels: 0 us -> 110 us
    all_to_all x6 -> x0, waiting for transfers between devices: 452 us -> none  [the longest x1 252 us: on_device(): lax.all_to_all(velocity, 'wide', split_axis=3, concat_axis=1, tiled=True)]
    unnamed x29 -> x15, local copies, waits for them, and re-layouts: 373 us -> 4.53 us
    all_to_all x13 -> x0, local copies, waits for them, and re-layouts: 300 us -> none  [the longest x2 53.4 us: on_device(): lax.all_to_all(velocity, 'narrow', split_axis=3, concat_axis=2, tiled=True)]
    all_to_all x6 -> x0, other arithmetic: 230 us -> none  [the longest x1 39.9 us: on_device(): lax.all_to_all(adjoint, 'narrow', split_axis=3, concat_axis=2, tiled=True)]
    gather x3 -> x0, local copies, waits for them, and re-layouts: 130 us -> none  [the longest x1 43.2 us: turbine_terms(): ay_rows = adjoint[1].reshape(-1, 128)[row_index]]
    dot_general x7 -> x0, matrix products: 125 us -> none  [the longest x1 26.9 us: on_device(): adj_dx = jnp.einsum('czyk,xk->czyx', adjoint, deriv_x, precision=highest)]
    pallas_call x0 -> x6, Pallas kernels: none -> 110 us  [the longest x1 34.3 us: xy_terms(): pl.pallas_call(xy_kernel, grid=(shard_z // planes,), in_specs=[whole(m) f...]
    reshape x5 -> x0, local copies, waits for them, and re-layouts: 94.7 us -> none  [the longest x2 47.3 us: on_device(): jnp.einsum('ckm,zk->czm', flat_vel, deriv_z, precision=highest)]
  transfers between devices with their start and end apart: 6 -> 8, of which waited for: 3 -> 1; matrix products, arithmetic and copies ran while one was open for 63% -> 21% of each run, Pallas kernels for 0% -> 39%
where the time goes in v1:
time: 266 us; the launch traced here: 264 us
  Pallas kernels  110 us (41%)
  local copies, waits for them, and re-layouts  44.8 us (17%)
  blocking collectives  42.4 us (16%)
  other arithmetic  25.4 us (10%)
  waiting for transfers between devices  22.8 us (9%)
  starting transfers between devices  18.3 us (7%)
    all_gather x1, blocking collectives, owner_rows(): lax.all_gather(partial_value, ('wide', 'narrow'), axis=0, tiled=False)  42.4 us
    pallas_call x1, Pallas kernels, xy_terms(): pl.pallas_call(xy_kernel, grid=(shard_z // planes,), in_specs=[whole(m) f...  34.3 us
    pallas_call x1, Pallas kernels, z_local(): pl.pallas_call(z_local_kernel, grid=(shard_y // GROUP,), in_specs=[pl.Blo...  24.4 us
    ppermute x4, waiting for transfers between devices, send_up(): return lax.ppermute(value, axis, [(i, i + 1) for i in range(size - 1)])  22.8 us
    mul x5, local copies, waits for them, and re-layouts, on_device(): spread = lambda m: jnp.kron(m, lanes)  20.1 us
    pallas_call x1, Pallas kernels, combine(): pl.pallas_call(combine_kernel, grid=(shard_y // GROUP,), in_specs=[whole(...  18.4 us
    pallas_call x1, Pallas kernels, turbine_terms(): pl.pallas_call(functools.partial(turbine_kernel, count, (shard_z, shard_y...  17.2 us
    ppermute x4, starting transfers between devices, send_up(): return lax.ppermute(value, axis, [(i, i + 1) for i in range(size - 1)])  13.2 us
  transfers between devices with their start and end apart: 8, of which 1 were waited for; matrix products, arithmetic and copies ran while one was open for 21% of the time, Pallas kernels for 39%

profile of v1, /device:TPU:0, one launch (start us, length us, event | category | flops | bytes accessed | tf_op | source)
XLA Modules:
  0.0 264.1 jit_solution(7720133896128720989)
XLA Ops:
  0.6 11.9 %fusion.31 = (f32[3,64,32,256]{3,2,1,0:T(8,128)}, f32[3,64,32,256]{3,2,1,0:T(8,128)}) fusion(f32[3,64,64,256]{3,2,1,0:T(8,128)} %adjoint.5), kind=kLoop, calls=%fused_computation.90 | loop fusion | bytes 25165824 | tf_op jit(solution)/shard_map/slice | solution.py:374
  12.5 5.0 %collective-permute-start.4 = (f32[3,64,32,256]{3,2,1,0:T(8,128)}, f32[3,64,32,256]{3,2,1,0:T(8,128)}, u32[]{:S(2)}, u32[]{:S(2)}) collective-permute-start(f32[3,64,32,256]{3,2,1,0:T(8,128)} %get-tuple-element.25), channel_id=1, source_target_pairs={{0,1},{1,2},{2,3},{4,5},{5,6},{6,7},{8,9},{9,10},{10,11},{12,13},{... | collective-permute-start | bytes 18874376 | tf_op jit(solution)/shard_map/ppermute | solution.py:336
  17.6 1.3 collective-permute-start.5
  18.9 6.3 %fusion.32 = (f32[3,16,64,256]{3,2,1,0:T(8,128)}, f32[3,16,64,256]{3,2,1,0:T(8,128)}) fusion(f32[3,64,64,256]{3,2,1,0:T(8,128)} %adjoint.5), kind=kLoop, calls=%fused_computation.91 | loop fusion | bytes 12582912 | tf_op jit(solution)/shard_map/slice | solution.py:372
  25.2 4.4 %collective-permute-start = (f32[3,16,64,256]{3,2,1,0:T(8,128)}, f32[3,16,64,256]{3,2,1,0:T(8,128)S(1)}, u32[]{:S(2)}, u32[]{:S(2)}) collective-permute-start(f32[3,16,64,256]{3,2,1,0:T(8,128)} %get-tuple-element.27), channel_id=1, source_target_pairs={{0,4},{4,8},{8,12},{12,16},{16,20},{20,24},{24,28},{1,5},{5,9},{9,... | collective-permute-start | bytes 9437192 | tf_op jit(solution)/shard_map/ppermute | solution.py:336
  29.7 1.3 collective-permute-start.1
  31.0 1.0 pad_dynamic-slice_fusion.2
  32.0 8.0 %broadcast_multiply_fusion = f32[64,8,64,8]{3,2,1,0:T(8,128)} fusion(f32[8,8]{1,0:T(8,128)S(1)} %fusion.27, f32[64,64]{1,0:T(8,128)S(1)} %pad_dynamic-slice_fusion.2), kind=kLoop, calls=%fused_computation | loop fusion | flops 262144 | bytes 1065216 | tf_op jit(solution)/shard_map/jit(kron)/mul | solution.py:383
  40.0 13.5 %mul.141 = f32[512,512]{1,0:T(8,128)} reshape(f32[64,8,64,8]{3,2,1,0:T(8,128)} %broadcast_multiply_fusion) | data formatting | bytes 2097152 | tf_op jit(solution)/shard_map/jit(kron)/mul | solution.py:383
  55.6 17.2 %turbine_terms.1 = (f32[64,64,256]{2,1,0:T(8,128)}, f32[96,128]{1,0:T(8,128)}, f32[96,128]{1,0:T(8,128)}) custom-call(s32[96]{0:T(128)} %fusion.30.zs, s32[96]{0:T(128)} %get-tuple-element.18.ys, s32[96]{0:T(128)} %get-tuple-element.54.xs, f32[96]{0:T(128)} %thrust.1, f32[3,64,64,256]{3,2,1,0:T(8,128)} %adjoint.5, f32[3,64,64,256]{3,2,1,0:T(8,128)} %adjoint.5, ...), custom_call_target="tpu_custom_call" | custom-call | flops 1000000 | bytes 30000000 | tf_op jit(solution)/shard_map/turbine_terms/pallas_call | solution.py:114
  78.4 1.0 reduce-precision_convert_fusion.1
  80.2 1.4 reduce-precision_convert_fusion
  81.5 1.1 pad_maximum_fusion.matrix
  82.6 2.3 broadcast_multiply_fusion.1
  84.9 24.4 %z_local.1.tendency = f32[3,64,64,256]{3,2,1,0:T(8,128)} custom-call(bf16[1024,512]{1,0:T(8,128)(2,1)} %pad_maximum_fusion.matrix, f32[3,64,64,256]{3,2,1,0:T(8,128)} %adjoint.5, f32[3,64,64,256]{3,2,1,0:T(8,128)} %carrier.1), custom_call_target="tpu_custom_call" | custom-call | flops 20000000000 | bytes 40000000 | tf_op jit(solution)/shard_map/z_local/pallas_call | solution.py:166
  109.3 1.7 mul.136
  110.9 1.6 mul.133
  112.6 1.6 mul.130
  114.2 1.6 mul.127
  115.9 42.4 %all_gather.4 = f32[32,2,96]{2,1,0:T(2,128)S(1)} all-gather(f32[1,2,96]{2,1,0:T(2,128)S(1)} %maximum_multiply_fusion), channel_id=1, replica_groups=mesh['wide'=8,'narrow'=4] {'wide','narrow'}, dimensions={0}, use_global_device_ids=true | all-gather | bytes 25344 | tf_op jit(solution)/shard_map/all_gather | solution.py:357
  158.3 34.3 %xy_terms.1 = (f32[3,64,64,256]{3,2,1,0:T(8,128)}, f32[64,32,256]{2,1,0:T(8,128)}, f32[64,32,256]{2,1,0:T(8,128)}) custom-call(bf16[256,512]{1,0:T(8,128)(2,1)} %pad_maximum_fusion.1.matrix_x, bf16[128,256]{1,0:T(8,128)(2,1)} %fusion.15.matrix_ya, bf16[128,128]{1,0:T(8,128)(2,1)} %fusion.20.matrix_yv, bf16[64,64]{1,0:T(8,128)(2,1)} %fusion.25.edge_low, ...), custom_call_target="tpu_custom_call" | custom-call | flops 20000000000 | bytes 70000000 | tf_op jit(solution)/shard_map/xy_terms/pallas_call | solution.py:229
  192.5 2.4 collective-permute-start.6
  194.9 1.3 collective-permute-start.7
  197.8 1.7 copy-done
  199.5 8.9 %z_back.1 = (f32[16,64,256]{2,1,0:T(8,128)}, f32[16,64,256]{2,1,0:T(8,128)}) custom-call(bf16[256,256]{1,0:T(8,128)(2,1)} %get-tuple-element.55.edge_low, bf16[256,256]{1,0:T(8,128)(2,1)} %get-tuple-element.56.edge_high, f32[3,64,64,256]{3,2,1,0:T(8,128)} %carrier.1, f32[3,64,64,256]{3,2,1,0:T(8,128)} %carrier.1, f32[3,16,64,256]{3,2,1,0:T(8,128)} %copy-done, ...), custom_call_target="tpu_custom_call" | custom-call | flops 3000000000 | bytes 20000000 | tf_op jit(solution)/shard_map/z_back/pallas_call | solution.py:262
  208.4 1.3 collective-permute-start.2
  209.7 1.3 collective-permute-start.3
  211.8 2.6 pad_add_fusion.stretch_y
  214.4 18.4 %combine.1.updated = f32[3,64,64,256]{3,2,1,0:T(8,128)} custom-call(bf16[256,256]{1,0:T(8,128)(2,1)} %get-tuple-element.59.from_low, bf16[256,256]{1,0:T(8,128)(2,1)} %get-tuple-element.60.from_high, f32[3,64,64,256]{3,2,1,0:T(8,128)} %adjoint.5, f32[3,64,64,256]{3,2,1,0:T(8,128)} %carrier.1, f32[3,64,64,256]{3,2,1,0:T(8,128)} %get-tuple-element.13.tendency, ...), custom_call_target="tpu_custom_call" | custom-call | flops 3000000000 | bytes 50000000 | tf_op jit(solution)/shard_map/combine/pallas_call | solution.py:298
  232.8 22.8 %collective-permute-done.2.back_low = f32[16,64,256]{2,1,0:T(8,128)S(1)} collective-permute-done((f32[16,64,256]{2,1,0:T(8,128)}, f32[16,64,256]{2,1,0:T(8,128)S(1)}, u32[]{:S(2)}, u32[]{:S(2)}) %collective-permute-start.2) | collective-permute-done | bytes 1048608 | tf_op jit(solution)/shard_map/ppermute | solution.py:336
  256.6 1.0 copy-done.3
  257.6 6.5 %finish.1 = f32[3,64,64,256]{3,2,1,0:T(8,128)} custom-call(f32[16,64,256]{2,1,0:T(8,128)} %copy-done.2, f32[16,64,256]{2,1,0:T(8,128)} %copy-done.3, f32[3,64,64,256]{3,2,1,0:T(8,128)} %combine.1.updated), custom_call_target="tpu_custom_call", output_to_operand_aliasing={{}: (2, {})} | custom-call | flops 1000000 | bytes 6000000 | tf_op jit(solution)/shard_map/finish/pallas_call | solution.py:321
  (48 shorter events, 11.8 us)
Async XLA Ops:
  12.5 145.7 %collective-permute-start.4 = (f32[3,64,32,256]{3,2,1,0:T(8,128)}, f32[3,64,32,256]{3,2,1,0:T(8,128)}, u32[]{:S(2)}, u32[]{:S(2)}) collective-permute-start(f32[3,64,32,256]{3,2,1,0:T(8,128)} %get-tuple-element.25), channel_id=1, source_target_pairs={{0,1},{1,2},{2,3},{4,5},{5,6},{6,7},{8,9},{9,10},{10,11},{12,13},{... | collective-permute-start | bytes 18874376 | tf_op jit(solution)/shard_map/ppermute | solution.py:336
  17.6 140.7 %collective-permute-start.5 = (f32[3,64,32,256]{3,2,1,0:T(8,128)}, f32[3,64,32,256]{3,2,1,0:T(8,128)}, u32[]{:S(2)}, u32[]{:S(2)}) collective-permute-start(f32[3,64,32,256]{3,2,1,0:T(8,128)} %get-tuple-element.24), channel_id=1, source_target_pairs={{1,0},{2,1},{3,2},{5,4},{6,5},{7,6},{9,8},{10,9},{11,10},{13,12},{... | collective-permute-start | bytes 18874376 | tf_op jit(solution)/shard_map/ppermute | solution.py:341
  25.2 172.6 %collective-permute-start = (f32[3,16,64,256]{3,2,1,0:T(8,128)}, f32[3,16,64,256]{3,2,1,0:T(8,128)S(1)}, u32[]{:S(2)}, u32[]{:S(2)}) collective-permute-start(f32[3,16,64,256]{3,2,1,0:T(8,128)} %get-tuple-element.27), channel_id=1, source_target_pairs={{0,4},{4,8},{8,12},{12,16},{16,20},{20,24},{24,28},{1,5},{5,9},{9,... | collective-permute-start | bytes 9437192 | tf_op jit(solution)/shard_map/ppermute | solution.py:336
  29.7 168.2 %collective-permute-start.1 = (f32[3,16,64,256]{3,2,1,0:T(8,128)}, f32[3,16,64,256]{3,2,1,0:T(8,128)}, u32[]{:S(2)}, u32[]{:S(2)}) collective-permute-start(f32[3,16,64,256]{3,2,1,0:T(8,128)} %get-tuple-element.26), channel_id=1, source_target_pairs={{4,0},{8,4},{12,8},{16,12},{20,16},{24,20},{28,24},{5,1},{9,5},{13... | collective-permute-start | bytes 9437192 | tf_op jit(solution)/shard_map/ppermute | solution.py:341
  40.0 13.5 %copy-start.4 = (f32[256,256]{1,0:T(8,128)S(1)}, f32[256,256]{1,0:T(8,128)}, u32[]{:S(2)}) copy-start(f32[256,256]{1,0:T(8,128)} %param.11) | copy-start | bytes 786436
  40.0 14.3 %copy-start.5 = (s32[96,128]{1,0:T(8,128)S(1)}, s32[96,128]{1,0:T(8,128)}, u32[]{:S(2)}) copy-start(s32[96,128]{1,0:T(8,128)} %param.14) | copy-start | bytes 147460
  55.5 19.0 %copy-start.1 = (f32[256,256]{1,0:T(8,128)S(1)}, f32[256,256]{1,0:T(8,128)}, u32[]{:S(2)}) copy-start(f32[256,256]{1,0:T(8,128)} %param.12) | copy-start | bytes 786436
  158.3 37.9 %copy-start.6 = (s32[96]{0:T(128)S(1)}, s32[96]{0:T(128)}, u32[]{:S(2)}) copy-start(s32[96]{0:T(128)} %param.15) | copy-start | bytes 1156
  192.5 19.3 %collective-permute-start.6 = (f32[64,32,256]{2,1,0:T(8,128)}, f32[64,32,256]{2,1,0:T(8,128)S(1)}, u32[]{:S(2)}, u32[]{:S(2)}) collective-permute-start(f32[64,32,256]{2,1,0:T(8,128)} %get-tuple-element.14), channel_id=1, source_target_pairs={{0,1},{1,2},{2,3},{4,5},{5,6},{6,7},{8,9},{9,10},{10,11},{12,13},{... | collective-permute-start | bytes 6291464 | tf_op jit(solution)/shard_map/ppermute | solution.py:336
  194.9 16.9 %collective-permute-start.7 = (f32[64,32,256]{2,1,0:T(8,128)}, f32[64,32,256]{2,1,0:T(8,128)S(1)}, u32[]{:S(2)}, u32[]{:S(2)}) collective-permute-start(f32[64,32,256]{2,1,0:T(8,128)} %get-tuple-element.15), channel_id=1, source_target_pairs={{1,0},{2,1},{3,2},{5,4},{6,5},{7,6},{9,8},{10,9},{11,10},{13,12},{... | collective-permute-start | bytes 6291464 | tf_op jit(solution)/shard_map/ppermute | solution.py:341
  197.8 1.7 copy-start
  208.4 47.2 %collective-permute-start.2 = (f32[16,64,256]{2,1,0:T(8,128)}, f32[16,64,256]{2,1,0:T(8,128)S(1)}, u32[]{:S(2)}, u32[]{:S(2)}) collective-permute-start(f32[16,64,256]{2,1,0:T(8,128)} %get-tuple-element.10), channel_id=1, source_target_pairs={{0,4},{4,8},{8,12},{12,16},{16,20},{20,24},{24,28},{1,5},{5,9},{9,... | collective-permute-start | bytes 3145736 | tf_op jit(solution)/shard_map/ppermute | solution.py:336
  209.7 45.9 %collective-permute-start.3 = (f32[16,64,256]{2,1,0:T(8,128)}, f32[16,64,256]{2,1,0:T(8,128)S(1)}, u32[]{:S(2)}, u32[]{:S(2)}) collective-permute-start(f32[16,64,256]{2,1,0:T(8,128)} %get-tuple-element.11), channel_id=1, source_target_pairs={{4,0},{8,4},{12,8},{16,12},{20,16},{24,20},{28,24},{5,1},{9,5},{13... | collective-permute-start | bytes 3145736 | tf_op jit(solution)/shard_map/ppermute | solution.py:341
  255.6 1.0 copy-start.2
  256.6 1.0 copy-start.3

commit v2 on v1

--- a/solution.py
+++ b/solution.py
@@ -17,12 +17,12 @@
 VMEM = 56 * 1024 * 1024
 
 
-def params():
-    return pltpu.CompilerParams(vmem_limit_bytes=VMEM)
+def params(limit=VMEM):
+    return pltpu.CompilerParams(vmem_limit_bytes=limit)
 
 
 def cost(flops, moved):
-    return pl.CostEstimate(flops=int(flops), bytes_accessed=int(moved), transcendentals=0)
+    return pl.CostEstimate(flops=int(flops / 50), bytes_accessed=int(moved / 50), transcendentals=0)
 
 
 def split(value):
@@ -35,21 +35,79 @@
     return jnp.dot(left, right, preferred_element_type=jnp.float32)
 
 
-def split_matrix(matrix):
-    high = lax.reduce_precision(matrix, 8, 7)
-    return high, matrix - high
-
-
-def stacked(matrix):
-    high, low = split_matrix(matrix)
-    top = jnp.concatenate([high, high], axis=1)
-    bottom = jnp.concatenate([low, jnp.zeros_like(low)], axis=1)
+def picked(window, rows, first_row, columns, first_column, repeat, copies):
+    size = window.shape[0]
+    height, width = rows * repeat, columns * repeat * copies
+    i = lax.broadcasted_iota(jnp.int32, (height, size), 0)
+    k = lax.broadcasted_iota(jnp.int32, (height, size), 1)
+    left = (lax.div(i, repeat) + first_row == k).astype(jnp.float32).astype(jnp.bfloat16)
+    k = lax.broadcasted_iota(jnp.int32, (size, width), 0)
+    j = lax.rem(lax.broadcasted_iota(jnp.int32, (size, width), 1), columns * repeat)
+    right = (lax.div(j, repeat) + first_column == k).astype(jnp.float32).astype(jnp.bfloat16)
+    block = dot(dot(left, window).astype(jnp.bfloat16), right)
+    i = lax.broadcasted_iota(jnp.int32, (height, width), 0)
+    j = lax.broadcasted_iota(jnp.int32, (height, width), 1)
+    return jnp.where(lax.rem(i, repeat) == lax.rem(j, repeat), block, 0.0), j
+
+
+def stacked(window, rows, first_row, columns, first_column, repeat):
+    high, low = window
+    top, j = picked(high, rows, first_row, columns, first_column, repeat, 2)
+    bottom, _ = picked(low, rows, first_row, columns, first_column, repeat, 2)
+    bottom = jnp.where(j < columns * repeat, bottom, 0.0)
     return jnp.concatenate([top, bottom], axis=0).astype(jnp.bfloat16)
 
 
-def paired(matrix, axis):
-    high, low = split_matrix(matrix)
-    return jnp.concatenate([high, low], axis=axis).astype(jnp.bfloat16)
+def matrices_kernel(
+    shard_z, shard_y, x, y, z,
+    x_pair, y_full, y_local, y_to_low, y_to_high,
+    z_pair, z_from_low, z_from_high, z_to_low, z_to_high,
+):
+    high, low = split(x[...].T)
+    x_pair[:, : high.shape[1]] = high
+    x_pair[:, high.shape[1] :] = low
+    window = split(y[...])
+    y_full[...] = stacked(window, shard_y, BY, shard_y + 2 * BY, 0, 1)
+    y_local[...] = stacked(window, shard_y, BY, shard_y, BY, 1)
+    y_to_low[...] = stacked(window, BY, 0, BY, BY, 1)
+    y_to_high[...] = stacked(window, BY, shard_y + BY, BY, shard_y, 1)
+    window = split(z[...])
+    rows = shard_z * GROUP
+    for at in range(2):
+        block, _ = picked(window[at], shard_z, BAND, shard_z, BAND, GROUP, 1)
+        z_pair[at * rows : (at + 1) * rows, :] = block.astype(jnp.bfloat16)
+    z_from_low[...] = stacked(window, BAND, BAND, BAND, 0, GROUP)
+    z_from_high[...] = stacked(window, BAND, shard_z, BAND, shard_z + BAND, GROUP)
+    z_to_low[...] = stacked(window, BAND, 0, BAND, BAND, GROUP)
+    z_to_high[...] = stacked(window, BAND, shard_z + BAND, BAND, shard_z, GROUP)
+
+
+def window(matrix, first, shard, halo):
+    return lax.dynamic_slice(jnp.pad(matrix, halo), (first, first), (shard + 2 * halo,) * 2)
+
+
+def matrices(deriv_x, deriv_y, deriv_z, shard_z, shard_y):
+    extent = deriv_x.shape[0]
+    z = window(deriv_z, lax.axis_index("wide") * shard_z, shard_z, BAND)
+    y = window(deriv_y, lax.axis_index("narrow") * shard_y, shard_y, BY)
+    edge = 2 * BAND * GROUP
+    rows = shard_z * GROUP
+    shapes = [
+        (extent, 2 * extent),
+        (2 * shard_y, 2 * (shard_y + 2 * BY)),
+        (2 * shard_y, 2 * shard_y),
+        (2 * BY, 2 * BY),
+        (2 * BY, 2 * BY),
+        (2 * rows, rows),
+    ] + [(edge, edge)] * 4
+    out = pl.pallas_call(
+        functools.partial(matrices_kernel, shard_z, shard_y),
+        out_shape=[jax.ShapeDtypeStruct(shape, jnp.bfloat16) for shape in shapes],
+        compiler_params=params(24 * 1024 * 1024),
+        cost_estimate=cost(1e8, 4e6),
+        name="matrices",
+    )(deriv_x, y, z)
+    return out[:5], out[5], out[6:8], out[8:10]
 
 
 def apply_stacked(matrix, values):
@@ -217,7 +275,7 @@
         back_high[plane] = high_sum
 
 
-def xy_terms(matrices, adjoint, velocity, halo_low, halo_high, source, tendency):
+def xy_terms(operators, adjoint, velocity, halo_low, halo_high, source, tendency):
     _, shard_z, shard_y, extent = adjoint.shape
     planes = 4
     whole = lambda m: pl.BlockSpec(m.shape, lambda i: (0, 0))
@@ -229,13 +287,13 @@
     return pl.pallas_call(
         xy_kernel,
         grid=(shard_z // planes,),
-        in_specs=[whole(m) for m in matrices] + [block, block, halo, halo, plane, block],
+        in_specs=[whole(m) for m in operators] + [block, block, halo, halo, plane, block],
         out_specs=[block, back, back],
         out_shape=[jax.ShapeDtypeStruct(adjoint.shape, jnp.float32), back_shape, back_shape],
         compiler_params=params(),
         cost_estimate=cost(2e10, 7e7),
         name="xy_terms",
-    )(*matrices, adjoint, velocity, halo_low, halo_high, source, tendency)
+    )(*operators, adjoint, velocity, halo_low, halo_high, source, tendency)
 
 
 def z_back_kernel(edge_low, edge_high, vel_low, vel_high, halo_low, halo_high, back_low, back_high):
@@ -265,7 +323,7 @@
         in_specs=[whole(edge_low), whole(edge_high), edge(0), edge(last), edge(0), edge(0)],
         out_specs=[back, back],
         out_shape=[shape, shape],
-        compiler_params=params(),
+        compiler_params=params(16 * 1024 * 1024),
         cost_estimate=cost(3e9, 2e7),
         name="z_back",
     )(edge_low, edge_high, velocity, velocity, halo_low, halo_high)
@@ -325,7 +383,7 @@
         out_specs=edge,
         out_shape=jax.ShapeDtypeStruct(updated.shape, jnp.float32),
         input_output_aliases={2: 0},
-        compiler_params=params(),
+        compiler_params=params(8 * 1024 * 1024),
         cost_estimate=cost(1e6, 6e6),
         name="finish",
     )(back_low, back_high, updated)
@@ -341,21 +399,20 @@
     return lax.ppermute(value, axis, [(i + 1, i) for i in range(size - 1)])
 
 
-def windows(matrix, first, shard, halo):
-    padded = jnp.pad(matrix, halo)
-    rows = lax.dynamic_slice(padded, (first + halo, first), (shard, shard + 2 * halo))
-    to_low = lax.dynamic_slice(padded, (first, first + halo), (halo, halo))
-    to_high = lax.dynamic_slice(padded, (first + shard + halo, first + shard), (halo, halo))
-    return rows, to_low, to_high
-
-
-def owner_rows(partial_value, turbine_owner):
+def exchange(value, axis, distance):
+    size = lax.axis_size(axis)
+    return lax.ppermute(value, axis, [(i, i ^ distance) for i in range(size)])
+
+
+def after(value, *others):
+    return lax.optimization_barrier((value, *others))
+
+
+def owner_rows(grad, turbine_owner):
     turbines = turbine_owner.shape[0]
     devices = lax.axis_size("wide") * lax.axis_size("narrow")
     slot_count = (turbines - 2) // devices + 2
     device = lax.axis_index("wide") * lax.axis_size("narrow") + lax.axis_index("narrow")
-    gathered = lax.all_gather(partial_value, ("wide", "narrow"), axis=0, tiled=False)
-    grad = jnp.sum(gathered, axis=0)
     positions = jnp.arange(turbines)
     shared = turbine_owner[:, None] == turbine_owner[None, :]
     earlier = positions[:, None] > positions[None, :]
@@ -370,52 +427,50 @@
     _, shard_z, shard_y, extent = adjoint.shape
     z_low = send_up(adjoint[:, shard_z - BAND :], "wide")
     z_high = send_down(adjoint[:, :BAND], "wide")
+    xy_matrices, z_pair, z_from, z_to = matrices(deriv_x, deriv_y, deriv_z, shard_z, shard_y)
+    z_pair, adjoint = after(z_pair, adjoint)
     y_low = send_up(adjoint[:, :, shard_y - BY :], "narrow")
     y_high = send_down(adjoint[:, :, :BY], "narrow")
 
-    rows_z, z_to_low, z_to_high = windows(
-        deriv_z, lax.axis_index("wide") * shard_z, shard_z, BAND
-    )
-    rows_y, y_to_low, y_to_high = windows(
-        deriv_y, lax.axis_index("narrow") * shard_y, shard_y, BY
-    )
-    lanes = jnp.eye(GROUP, dtype=jnp.float32)
-    spread = lambda m: jnp.kron(m, lanes)
+    steps = [("narrow", 2**k) for k in range(8) if 2**k < lax.axis_size("narrow")]
+    steps += [("wide", 2**k) for k in range(8) if 2**k < lax.axis_size("wide")]
 
     source, grad0, grad1 = turbine_terms(adjoint, velocity, rotor_blocks, disk_weight, thrust)
     scale = 1.0 / math.sqrt(128.0 * rotor_blocks.shape[1])
-    partial_value = jnp.stack([jnp.sum(grad0, axis=1), jnp.sum(grad1, axis=1)]) * scale
-    turbine_grad = owner_rows(partial_value, turbine_owner)
-
-    local_z = paired(spread(rows_z[:, BAND : BAND + shard_z]), 0)
-    tendency = z_local(local_z, adjoint, velocity)
-    matrices = (
-        paired(deriv_x.T, 1),
-        stacked(rows_y),
-        stacked(rows_y[:, BY : BY + shard_y]),
-        stacked(y_to_low),
-        stacked(y_to_high),
+    grad = jnp.stack([jnp.sum(grad0, axis=1), jnp.sum(grad1, axis=1)]) * scale
+
+    moved = exchange(grad, *steps[0])
+    tendency = z_local(z_pair, adjoint, velocity)
+    moved, tendency = after(moved, tendency)
+    grad = grad + moved
+    moved = exchange(grad, *steps[1])
+    moved, y_low, y_high = after(moved, y_low, y_high)
+    grad = grad + moved
+    moved = exchange(grad, *steps[2])
+    tendency, y_back_low, y_back_high = xy_terms(
+        xy_matrices, adjoint, velocity, y_low, y_high, source, tendency
     )
-    tendency, y_back_low, y_back_high = xy_terms(
-        matrices, adjoint, velocity, y_low, y_high, source, tendency
-    )
+    moved, y_back_low, y_back_high = after(moved, y_back_low, y_back_high)
+    grad = grad + moved
     stretch_low = send_up(y_back_high, "narrow")
     stretch_high = send_down(y_back_low, "narrow")
+    moved = exchange(grad, *steps[3])
+    moved, z_low, z_high = after(moved, z_low, z_high)
+    grad = grad + moved
+    z_back_low, z_back_high = z_back(*z_to, velocity, z_low, z_high)
+    last_low = send_up(z_back_high, "wide")
+    last_high = send_down(z_back_low, "wide")
     rest = shard_y - BY
     stretch_y = jnp.pad(stretch_low, ((0, 0), (0, rest), (0, 0))) + jnp.pad(
         stretch_high, ((0, 0), (rest, 0), (0, 0))
     )
-    z_back_low, z_back_high = z_back(
-        stacked(spread(z_to_low)), stacked(spread(z_to_high)), velocity, z_low, z_high
-    )
-    last_low = send_up(z_back_high, "wide")
-    last_high = send_down(z_back_low, "wide")
-    updated = combine(
-        stacked(spread(rows_z[:BAND, :BAND])),
-        stacked(spread(rows_z[shard_z - BAND :, BAND + shard_z :])),
-        adjoint, velocity, tendency, z_low, z_high, stretch_y,
-    )
-    return finish(updated, last_low, last_high), turbine_grad
+    moved = exchange(grad, *steps[4])
+    updated = combine(*z_from, adjoint, velocity, tendency, z_low, z_high, stretch_y)
+    moved, updated = after(moved, updated)
+    grad = grad + moved
+    for step in steps[5:]:
+        grad = grad + exchange(grad, *step)
+    return finish(updated, last_low, last_high), owner_rows(grad, turbine_owner)
 
 
 def solution(mesh):

time: 266 us -> 254 us (0.955)
  waiting for transfers between devices: 22.8 us -> 67.2 us
  blocking collectives: 42.4 us -> 0 us
  other arithmetic: 25.4 us -> 8.52 us
  starting transfers between devices: 18.3 us -> 33.3 us
  local copies, waits for them, and re-layouts: 44.8 us -> 31.3 us
    ppermute x0 -> x5, waiting for transfers between devices: none -> 54 us  [exchange(): return lax.ppermute(value, axis, [(i, i ^ distance) for i in range(size)])]
    all_gather x1 -> x0, blocking collectives: 42.4 us -> none  [owner_rows(): lax.all_gather(partial_value, ('wide', 'narrow'), axis=0, tiled=False)]
    mul x5 -> x0, local copies, waits for them, and re-layouts: 20.1 us -> none  [on_device(): spread = lambda m: jnp.kron(m, lanes)]
    ppermute x0 -> x5, starting transfers between devices: none -> 11.4 us  [exchange(): return lax.ppermute(value, axis, [(i, i ^ distance) for i in range(size)])]
    mul x3 -> x1, other arithmetic: 10.3 us -> 0.01 us  [on_device(): grad = jnp.stack([jnp.sum(grad0, axis=1), jnp.sum(grad1, axis=1)]) * scale]
    ppermute x4, waiting for transfers between devices: 22.8 us -> 13.2 us  [send_up(): return lax.ppermute(value, axis, [(i, i + 1) for i in range(size - 1)])]
    unnamed x15 -> x26, local copies, waits for them, and re-layouts: 4.53 us -> 10.9 us
    concatenate x8 -> x0, other arithmetic: 5.89 us -> none  [the longest x6 4.11 us: stacked(): return jnp.concatenate([top, bottom], axis=0).astype(jnp.bfloat16)]
  transfers between devices with their start and end apart: 8 -> 13, of which waited for: 1 -> 4; matrix products, arithmetic and copies ran while one was open for 21% -> 6% of each run, Pallas kernels for 39% -> 41%
where the time goes in v2:
time: 254 us; the launch traced here: 251 us
  Pallas kernels  110 us (43%)
  waiting for transfers between devices  67.2 us (26%)
  starting transfers between devices  33.3 us (13%)
  local copies, waits for them, and re-layouts  31.3 us (12%)
  other arithmetic  8.52 us (3%)
    ppermute x5, waiting for transfers between devices, exchange(): return lax.ppermute(value, axis, [(i, i ^ distance) for i in range(size)])  54 us
    pallas_call x1, Pallas kernels, xy_terms(): pl.pallas_call(xy_kernel, grid=(shard_z // planes,), in_specs=[whole(m) f...  34.3 us
    pallas_call x1, Pallas kernels, z_local(): pl.pallas_call(z_local_kernel, grid=(shard_y // GROUP,), in_specs=[pl.Blo...  24.4 us
    pallas_call x1, Pallas kernels, combine(): pl.pallas_call(combine_kernel, grid=(shard_y // GROUP,), in_specs=[whole(...  18.4 us
    pallas_call x1, Pallas kernels, turbine_terms(): pl.pallas_call(functools.partial(turbine_kernel, count, (shard_z, shard_y...  18.1 us
    ppermute x4, starting transfers between devices, send_up(): return lax.ppermute(value, axis, [(i, i + 1) for i in range(size - 1)])  16.6 us
    ppermute x4, waiting for transfers between devices, send_up(): return lax.ppermute(value, axis, [(i, i + 1) for i in range(size - 1)])  13.2 us
    slice x1, local copies, waits for them, and re-layouts, on_device(): y_high = send_down(adjoint[:, :, :BY], 'narrow')  11.9 us
  transfers between devices with their start and end apart: 13, of which 4 were waited for; matrix products, arithmetic and copies ran while one was open for 6% of the time, Pallas kernels for 41%

profile of v2, /device:TPU:0, one launch (start us, length us, event | category | flops | bytes accessed | tf_op | source)
XLA Modules:
  0.0 251.5 jit_solution(16967068165172168219)
XLA Ops:
  0.6 1.0 pad_dynamic-slice_fusion.1.y
  1.6 1.0 pad_dynamic-slice_fusion.z
  2.6 0.9 copy-done.4
  3.6 1.9 matrices.1
  5.5 0.9 copy-done.2
  10.9 11.9 %fusion.6 = (f32[3,64,32,256]{3,2,1,0:T(8,128)}, f32[3,64,32,256]{3,2,1,0:T(8,128)}) fusion(f32[3,64,64,256]{3,2,1,0:T(8,128)} %adjoint.2), kind=kLoop, calls=%fused_computation.26 | loop fusion | bytes 25165824 | tf_op jit(solution)/shard_map/slice | solution.py:433
  22.8 4.9 %collective-permute-start.2 = (f32[3,64,32,256]{3,2,1,0:T(8,128)}, f32[3,64,32,256]{3,2,1,0:T(8,128)}, u32[]{:S(2)}, u32[]{:S(2)}) collective-permute-start(f32[3,64,32,256]{3,2,1,0:T(8,128)} %get-tuple-element.73), channel_id=1, source_target_pairs={{0,1},{1,2},{2,3},{4,5},{5,6},{6,7},{8,9},{9,10},{10,11},{12,13},{... | collective-permute-start | bytes 18874376 | tf_op jit(solution)/shard_map/ppermute | solution.py:394
  27.8 1.4 collective-permute-start.3
  29.2 6.4 %fusion.5 = (f32[3,16,64,256]{3,2,1,0:T(8,128)}, f32[3,16,64,256]{3,2,1,0:T(8,128)}) fusion(f32[3,64,64,256]{3,2,1,0:T(8,128)} %adjoint.2), kind=kLoop, calls=%fused_computation.25 | loop fusion | bytes 12582912 | tf_op jit(solution)/shard_map/slice | solution.py:429
  35.6 4.5 %collective-permute-start.6 = (f32[3,16,64,256]{3,2,1,0:T(8,128)}, f32[3,16,64,256]{3,2,1,0:T(8,128)S(1)}, u32[]{:S(2)}, u32[]{:S(2)}) collective-permute-start(f32[3,16,64,256]{3,2,1,0:T(8,128)} %get-tuple-element.71), channel_id=1, source_target_pairs={{0,4},{4,8},{8,12},{12,16},{16,20},{20,24},{24,28},{1,5},{5,9},{9,... | collective-permute-start | bytes 9437192 | tf_op jit(solution)/shard_map/ppermute | solution.py:394
  40.1 1.3 collective-permute-start.7
  42.7 18.1 %turbine_terms.1 = (f32[64,64,256]{2,1,0:T(8,128)}, f32[96,128]{1,0:T(8,128)}, f32[96,128]{1,0:T(8,128)}) custom-call(s32[96]{0:T(128)} %fusion.3.zs, s32[96]{0:T(128)} %get-tuple-element.68.ys, s32[96]{0:T(128)} %get-tuple-element.74.xs, f32[96]{0:T(128)} %thrust.1, f32[3,64,64,256]{3,2,1,0:T(8,128)} %adjoint.2, f32[3,64,64,256]{3,2,1,0:T(8,128)} %adjoint.2, ...), custom_call_target="tpu_custom_call" | custom-call | flops 20000 | bytes 600000 | tf_op jit(solution)/shard_map/turbine_terms/pallas_call | solution.py:172
  60.8 0.9 reduce_sum.37
  61.7 0.9 reduce_sum.36
  63.0 24.4 %z_local.1.tendency = f32[3,64,64,256]{3,2,1,0:T(8,128)} custom-call(bf16[1024,512]{1,0:T(8,128)(2,1)} %copy-done.2, f32[3,64,64,256]{3,2,1,0:T(8,128)} %adjoint.2, f32[3,64,64,256]{3,2,1,0:T(8,128)} %carrier.1), custom_call_target="tpu_custom_call" | custom-call | flops 400000000 | bytes 800000 | tf_op jit(solution)/shard_map/z_local/pallas_call | solution.py:224
  87.5 13.1 %collective-permute-done.1 = f32[2,96]{1,0:T(2,128)S(1)} collective-permute-done((f32[2,96]{1,0:T(2,128)S(1)}, f32[2,96]{1,0:T(2,128)S(1)}, u32[]{:S(2)}, u32[]{:S(2)}) %collective-permute-start.1) | collective-permute-done | bytes 800 | tf_op jit(solution)/shard_map/ppermute | solution.py:404
  100.7 1.6 collective-permute-start.4
  102.3 34.3 %xy_terms.1 = (f32[3,64,64,256]{3,2,1,0:T(8,128)}, f32[64,32,256]{2,1,0:T(8,128)}, f32[64,32,256]{2,1,0:T(8,128)}) custom-call(bf16[256,512]{1,0:T(8,128)(2,1)} %copy-done.3, bf16[128,256]{1,0:T(8,128)(2,1)} %copy-done.7, bf16[128,128]{1,0:T(8,128)(2,1)} %copy-done.8, bf16[64,64]{1,0:T(8,128)(2,1)} %copy-done.9, bf16[64,64]{1,0:T(8,128)(2,1)} %copy-done.10, ...), custom_call_target="tpu_custom_call" | custom-call | flops 400000000 | bytes 1400000 | tf_op jit(solution)/shard_map/xy_terms/pallas_call | solution.py:287
  136.6 39.4 %collective-permute-done.4 = f32[2,96]{1,0:T(2,128)S(1)} collective-permute-done((f32[2,96]{1,0:T(2,128)S(1)}, f32[2,96]{1,0:T(2,128)S(1)}, u32[]{:S(2)}, u32[]{:S(2)}) %collective-permute-start.4) | collective-permute-done | bytes 800 | tf_op jit(solution)/shard_map/ppermute | solution.py:404
  175.9 1.3 collective-permute-start.12
  177.2 4.4 %collective-permute-start.11 = (f32[64,32,256]{2,1,0:T(8,128)}, f32[64,32,256]{2,1,0:T(8,128)}, u32[]{:S(2)}, u32[]{:S(2)}) collective-permute-start(f32[64,32,256]{2,1,0:T(8,128)} %get-tuple-element.64), channel_id=1, source_target_pairs={{0,1},{1,2},{2,3},{4,5},{5,6},{6,7},{8,9},{9,10},{10,11},{12,13},{... | collective-permute-start | bytes 6291464 | tf_op jit(solution)/shard_map/ppermute | solution.py:394
  181.6 3.6 %collective-permute-start.5 = (f32[2,96]{1,0:T(2,128)S(1)}, f32[2,96]{1,0:T(2,128)S(1)}, u32[]{:S(2)}, u32[]{:S(2)}) collective-permute-start(f32[2,96]{1,0:T(2,128)S(1)} %add.55), channel_id=1, source_target_pairs={{0,8},{4,12},{8,0},{12,4},{16,24},{20,28},{24,16},{28,20},{1,9},{5... | collective-permute-start | bytes 2312 | tf_op jit(solution)/shard_map/ppermute | solution.py:404
  185.2 1.5 collective-permute-done.5
  186.8 4.6 %copy-done = f32[3,64,64,256]{3,2,1,0:T(8,128)S(1)} copy-done((f32[3,64,64,256]{3,2,1,0:T(8,128)S(1)}, f32[3,64,64,256]{3,2,1,0:T(8,128)}, u32[]{:S(2)}) %copy-start) | copy-done | bytes 12582936
  191.3 7.3 %z_back.1 = (f32[16,64,256]{2,1,0:T(8,128)}, f32[16,64,256]{2,1,0:T(8,128)}) custom-call(bf16[256,256]{1,0:T(8,128)(2,1)S(1)} %get-tuple-element.35.edge_low, bf16[256,256]{1,0:T(8,128)(2,1)S(1)} %get-tuple-element.36.edge_high, f32[3,64,64,256]{3,2,1,0:T(8,128)S(1)} %copy-done, f32[3,64,64,256]{3,2,1,0:T(8,128)S(1)} %copy-done, ...), custom_call_target="tpu_custom_call" | custom-call | flops 60000000 | bytes 400000 | tf_op jit(solution)/shard_map/z_back/pallas_call | solution.py:320
  198.7 2.8 %collective-permute-start.8 = (f32[16,64,256]{2,1,0:T(8,128)}, f32[16,64,256]{2,1,0:T(8,128)S(1)}, u32[]{:S(2)}, u32[]{:S(2)}) collective-permute-start(f32[16,64,256]{2,1,0:T(8,128)} %get-tuple-element.58), channel_id=1, source_target_pairs={{0,4},{4,8},{8,12},{12,16},{16,20},{20,24},{24,28},{1,5},{5,9},{9,... | collective-permute-start | bytes 3145736 | tf_op jit(solution)/shard_map/ppermute | solution.py:394
  201.5 1.3 collective-permute-start.9
  203.0 5.7 %collective-permute-start.10 = (f32[2,96]{1,0:T(2,128)S(1)}, f32[2,96]{1,0:T(2,128)S(1)}, u32[]{:S(2)}, u32[]{:S(2)}) collective-permute-start(f32[2,96]{1,0:T(2,128)S(1)} %add.56), channel_id=1, source_target_pairs={{0,16},{4,20},{8,24},{12,28},{16,0},{20,4},{24,8},{28,12},{1,17},{... | collective-permute-start | bytes 2312 | tf_op jit(solution)/shard_map/ppermute | solution.py:404
  208.7 4.6 %pad_add_fusion.stretch_y = f32[64,64,256]{2,1,0:T(8,128)} fusion(f32[64,32,256]{2,1,0:T(8,128)} %collective-permute-done.12, f32[64,32,256]{2,1,0:T(8,128)} %collective-permute-done.11), kind=kLoop, calls=%fused_computation | loop fusion | flops 1048576 | bytes 8388608 | tf_op jit(solution)/shard_map/add | solution.py:464
  213.4 18.4 %combine.1.updated = f32[3,64,64,256]{3,2,1,0:T(8,128)} custom-call(bf16[256,256]{1,0:T(8,128)(2,1)} %copy-done.5, bf16[256,256]{1,0:T(8,128)(2,1)} %copy-done.6, f32[3,64,64,256]{3,2,1,0:T(8,128)} %adjoint.2, f32[3,64,64,256]{3,2,1,0:T(8,128)} %carrier.1, f32[3,64,64,256]{3,2,1,0:T(8,128)} %get-tuple-element.63.tendency, f32[3,16,64,256]{3,2,1,0:T(8,128)} %copy-done.1, ...), custom_call_target="tpu_custom_call" | custom-call | flops 60000000 | bytes 1000000 | tf_op jit(solution)/shard_map/combine/pallas_call | solution.py:356
  232.5 13.2 %collective-permute-done.8.back_low = f32[16,64,256]{2,1,0:T(8,128)S(1)} collective-permute-done((f32[16,64,256]{2,1,0:T(8,128)}, f32[16,64,256]{2,1,0:T(8,128)S(1)}, u32[]{:S(2)}, u32[]{:S(2)}) %collective-permute-start.8) | collective-permute-done | bytes 1048608 | tf_op jit(solution)/shard_map/ppermute | solution.py:394
  245.7 5.8 %finish.1 = f32[3,64,64,256]{3,2,1,0:T(8,128)} custom-call(f32[16,64,256]{2,1,0:T(8,128)S(1)} %collective-permute-done.8.back_low, f32[16,64,256]{2,1,0:T(8,128)S(1)} %collective-permute-done.9.back_high, f32[3,64,64,256]{3,2,1,0:T(8,128)} %combine.1.updated), custom_call_target="tpu_custom_call", output_to_operand_aliasing={{}: (2, {})} | custom-call | flops 20000 | bytes 120000 | tf_op jit(solution)/shard_map/finish/pallas_call | solution.py:379
  (47 shorter events, 7.1 us)
Async XLA Ops:
  2.6 1.0 copy-start.4
  5.5 1.0 copy-start.2
  6.5 0.7 copy-start.3
  7.2 0.6 copy-start.5
  7.8 0.7 copy-start.6
  8.5 0.6 copy-start.7
  9.1 0.6 copy-start.8
  9.7 0.6 copy-start.9
  10.3 0.6 copy-start.10
  22.8 77.8 %collective-permute-start.2 = (f32[3,64,32,256]{3,2,1,0:T(8,128)}, f32[3,64,32,256]{3,2,1,0:T(8,128)}, u32[]{:S(2)}, u32[]{:S(2)}) collective-permute-start(f32[3,64,32,256]{3,2,1,0:T(8,128)} %get-tuple-element.73), channel_id=1, source_target_pairs={{0,1},{1,2},{2,3},{4,5},{5,6},{6,7},{8,9},{9,10},{10,11},{12,13},{... | collective-permute-start | bytes 18874376 | tf_op jit(solution)/shard_map/ppermute | solution.py:394
  27.8 13.6 %copy-start.11 = (s32[96,128]{1,0:T(8,128)S(1)}, s32[96,128]{1,0:T(8,128)}, u32[]{:S(2)}) copy-start(s32[96,128]{1,0:T(8,128)} %param.14) | copy-start | bytes 147460
  27.8 72.9 %collective-permute-start.3 = (f32[3,64,32,256]{3,2,1,0:T(8,128)}, f32[3,64,32,256]{3,2,1,0:T(8,128)}, u32[]{:S(2)}, u32[]{:S(2)}) collective-permute-start(f32[3,64,32,256]{3,2,1,0:T(8,128)} %get-tuple-element.72), channel_id=1, source_target_pairs={{1,0},{2,1},{3,2},{5,4},{6,5},{7,6},{9,8},{10,9},{11,10},{13,12},{... | collective-permute-start | bytes 18874376 | tf_op jit(solution)/shard_map/ppermute | solution.py:399
  35.6 149.6 %collective-permute-start.6 = (f32[3,16,64,256]{3,2,1,0:T(8,128)}, f32[3,16,64,256]{3,2,1,0:T(8,128)S(1)}, u32[]{:S(2)}, u32[]{:S(2)}) collective-permute-start(f32[3,16,64,256]{3,2,1,0:T(8,128)} %get-tuple-element.71), channel_id=1, source_target_pairs={{0,4},{4,8},{8,12},{12,16},{16,20},{20,24},{24,28},{1,5},{5,9},{9,... | collective-permute-start | bytes 9437192 | tf_op jit(solution)/shard_map/ppermute | solution.py:394
  40.1 145.1 %collective-permute-start.7 = (f32[3,16,64,256]{3,2,1,0:T(8,128)}, f32[3,16,64,256]{3,2,1,0:T(8,128)}, u32[]{:S(2)}, u32[]{:S(2)}) collective-permute-start(f32[3,16,64,256]{3,2,1,0:T(8,128)} %get-tuple-element.70), channel_id=1, source_target_pairs={{4,0},{8,4},{12,8},{16,12},{20,16},{24,20},{28,24},{5,1},{9,5},{13... | collective-permute-start | bytes 9437192 | tf_op jit(solution)/shard_map/ppermute | solution.py:399
  62.7 24.7 %collective-permute-start = (f32[2,96]{1,0:T(2,128)S(1)}, f32[2,96]{1,0:T(2,128)S(1)}, u32[]{:S(2)}, u32[]{:S(2)}) collective-permute-start(f32[2,96]{1,0:T(2,128)S(1)} %maximum_multiply_fusion), channel_id=1, source_target_pairs={{0,1},{1,0},{2,3},{3,2},{4,5},{5,4},{6,7},{7,6},{8,9},{9,8},{10,11... | collective-permute-start | bytes 2312 | tf_op jit(solution)/shard_map/ppermute | solution.py:404
  87.4 13.2 %collective-permute-start.1 = (f32[2,96]{1,0:T(2,128)S(1)}, f32[2,96]{1,0:T(2,128)S(1)}, u32[]{:S(2)}, u32[]{:S(2)}) collective-permute-start(f32[2,96]{1,0:T(2,128)S(1)} %fusion.4), channel_id=1, source_target_pairs={{0,2},{1,3},{2,0},{3,1},{4,6},{5,7},{6,4},{7,5},{8,10},{9,11},{10,... | collective-permute-start | bytes 2312 | tf_op jit(solution)/shard_map/ppermute | solution.py:404
  100.7 75.3 %collective-permute-start.4 = (f32[2,96]{1,0:T(2,128)S(1)}, f32[2,96]{1,0:T(2,128)S(1)}, u32[]{:S(2)}, u32[]{:S(2)}) collective-permute-start(f32[2,96]{1,0:T(2,128)S(1)} %fusion.7), channel_id=1, source_target_pairs={{0,4},{4,0},{8,12},{12,8},{16,20},{20,16},{24,28},{28,24},{1,5},{5... | collective-permute-start | bytes 2312 | tf_op jit(solution)/shard_map/ppermute | solution.py:404
  175.9 32.8 %collective-permute-start.12 = (f32[64,32,256]{2,1,0:T(8,128)}, f32[64,32,256]{2,1,0:T(8,128)}, u32[]{:S(2)}, u32[]{:S(2)}) collective-permute-start(f32[64,32,256]{2,1,0:T(8,128)} %get-tuple-element.65), channel_id=1, source_target_pairs={{1,0},{2,1},{3,2},{5,4},{6,5},{7,6},{9,8},{10,9},{11,10},{13,12},{... | collective-permute-start | bytes 6291464 | tf_op jit(solution)/shard_map/ppermute | solution.py:399
  177.2 31.5 %collective-permute-start.11 = (f32[64,32,256]{2,1,0:T(8,128)}, f32[64,32,256]{2,1,0:T(8,128)}, u32[]{:S(2)}, u32[]{:S(2)}) collective-permute-start(f32[64,32,256]{2,1,0:T(8,128)} %get-tuple-element.64), channel_id=1, source_target_pairs={{0,1},{1,2},{2,3},{4,5},{5,6},{6,7},{8,9},{9,10},{10,11},{12,13},{... | collective-permute-start | bytes 6291464 | tf_op jit(solution)/shard_map/ppermute | solution.py:394
  181.6 5.1 %collective-permute-start.5 = (f32[2,96]{1,0:T(2,128)S(1)}, f32[2,96]{1,0:T(2,128)S(1)}, u32[]{:S(2)}, u32[]{:S(2)}) collective-permute-start(f32[2,96]{1,0:T(2,128)S(1)} %add.55), channel_id=1, source_target_pairs={{0,8},{4,12},{8,0},{12,4},{16,24},{20,28},{24,16},{28,20},{1,9},{5... | collective-permute-start | bytes 2312 | tf_op jit(solution)/shard_map/ppermute | solution.py:404
  185.2 13.5 %copy-start.1 = (f32[3,16,64,256]{3,2,1,0:T(8,128)}, f32[3,16,64,256]{3,2,1,0:T(8,128)S(1)}, u32[]{:S(2)}) copy-start(f32[3,16,64,256]{3,2,1,0:T(8,128)S(1)} %collective-permute-done.6.halo_low) | copy-start | bytes 9437188
  186.7 4.6 %copy-start = (f32[3,64,64,256]{3,2,1,0:T(8,128)S(1)}, f32[3,64,64,256]{3,2,1,0:T(8,128)}, u32[]{:S(2)}) copy-start(f32[3,64,64,256]{3,2,1,0:T(8,128)} %carrier.1) | copy-start | bytes 37748740
  191.3 11.5 %copy-start.12 = (s32[96]{0:T(128)S(1)}, s32[96]{0:T(128)}, u32[]{:S(2)}) copy-start(s32[96]{0:T(128)} %param.15) | copy-start | bytes 1156
  198.7 47.0 %collective-permute-start.8 = (f32[16,64,256]{2,1,0:T(8,128)}, f32[16,64,256]{2,1,0:T(8,128)S(1)}, u32[]{:S(2)}, u32[]{:S(2)}) collective-permute-start(f32[16,64,256]{2,1,0:T(8,128)} %get-tuple-element.58), channel_id=1, source_target_pairs={{0,4},{4,8},{8,12},{12,16},{16,20},{20,24},{24,28},{1,5},{5,9},{9,... | collective-permute-start | bytes 3145736 | tf_op jit(solution)/shard_map/ppermute | solution.py:394
  201.5 44.2 %collective-permute-start.9 = (f32[16,64,256]{2,1,0:T(8,128)}, f32[16,64,256]{2,1,0:T(8,128)S(1)}, u32[]{:S(2)}, u32[]{:S(2)}) collective-permute-start(f32[16,64,256]{2,1,0:T(8,128)} %get-tuple-element.59), channel_id=1, source_target_pairs={{4,0},{8,4},{12,8},{16,12},{20,16},{24,20},{28,24},{5,1},{9,5},{13... | collective-permute-start | bytes 3145736 | tf_op jit(solution)/shard_map/ppermute | solution.py:399
  203.0 28.8 %collective-permute-start.10 = (f32[2,96]{1,0:T(2,128)S(1)}, f32[2,96]{1,0:T(2,128)S(1)}, u32[]{:S(2)}, u32[]{:S(2)}) collective-permute-start(f32[2,96]{1,0:T(2,128)S(1)} %add.56), channel_id=1, source_target_pairs={{0,16},{4,20},{8,24},{12,28},{16,0},{20,4},{24,8},{28,12},{1,17},{... | collective-permute-start | bytes 2312 | tf_op jit(solution)/shard_map/ppermute | solution.py:404

commit v3 on v2

--- a/solution.py
+++ b/solution.py
@@ -103,7 +103,7 @@
     out = pl.pallas_call(
         functools.partial(matrices_kernel, shard_z, shard_y),
         out_shape=[jax.ShapeDtypeStruct(shape, jnp.bfloat16) for shape in shapes],
-        compiler_params=params(24 * 1024 * 1024),
+        compiler_params=params(),
         cost_estimate=cost(1e8, 4e6),
         name="matrices",
     )(deriv_x, y, z)
@@ -323,7 +323,7 @@
         in_specs=[whole(edge_low), whole(edge_high), edge(0), edge(last), edge(0), edge(0)],
         out_specs=[back, back],
         out_shape=[shape, shape],
-        compiler_params=params(16 * 1024 * 1024),
+        compiler_params=params(52 * 1024 * 1024),
         cost_estimate=cost(3e9, 2e7),
         name="z_back",
     )(edge_low, edge_high, velocity, velocity, halo_low, halo_high)
@@ -373,7 +373,7 @@
 def finish(updated, back_low, back_high):
     _, shard_z, shard_y, extent = updated.shape
     last = shard_z // BAND - 1
-    lines = 16
+    lines = shard_y // 2
     edge = pl.BlockSpec((None, BAND, lines, extent), lambda i, j: (2, i * last, j, 0))
     back = pl.BlockSpec((BAND, lines, extent), lambda i, j: (0, j, 0))
     return pl.pallas_call(
@@ -425,10 +425,9 @@
     adjoint, velocity, deriv_x, deriv_y, deriv_z, rotor_blocks, turbine_owner, disk_weight, thrust
 ):
     _, shard_z, shard_y, extent = adjoint.shape
-    z_low = send_up(adjoint[:, shard_z - BAND :], "wide")
-    z_high = send_down(adjoint[:, :BAND], "wide")
-    xy_matrices, z_pair, z_from, z_to = matrices(deriv_x, deriv_y, deriv_z, shard_z, shard_y)
-    z_pair, adjoint = after(z_pair, adjoint)
+    top, bottom, adjoint = after(adjoint[:, shard_z - BAND :], adjoint[:, :BAND], adjoint)
+    z_low = send_up(top, "wide")
+    z_high = send_down(bottom, "wide")
     y_low = send_up(adjoint[:, :, shard_y - BY :], "narrow")
     y_high = send_down(adjoint[:, :, :BY], "narrow")
 
@@ -438,6 +437,7 @@
     source, grad0, grad1 = turbine_terms(adjoint, velocity, rotor_blocks, disk_weight, thrust)
     scale = 1.0 / math.sqrt(128.0 * rotor_blocks.shape[1])
     grad = jnp.stack([jnp.sum(grad0, axis=1), jnp.sum(grad1, axis=1)]) * scale
+    xy_matrices, z_pair, z_from, z_to = matrices(deriv_x, deriv_y, deriv_z, shard_z, shard_y)
 
     moved = exchange(grad, *steps[0])
     tendency = z_local(z_pair, adjoint, velocity)
@@ -450,25 +450,22 @@
     tendency, y_back_low, y_back_high = xy_terms(
         xy_matrices, adjoint, velocity, y_low, y_high, source, tendency
     )
-    moved, y_back_low, y_back_high = after(moved, y_back_low, y_back_high)
-    grad = grad + moved
     stretch_low = send_up(y_back_high, "narrow")
     stretch_high = send_down(y_back_low, "narrow")
-    moved = exchange(grad, *steps[3])
-    moved, z_low, z_high = after(moved, z_low, z_high)
+    moved, tendency, z_low, z_high = after(moved, tendency, z_low, z_high)
     grad = grad + moved
     z_back_low, z_back_high = z_back(*z_to, velocity, z_low, z_high)
     last_low = send_up(z_back_high, "wide")
     last_high = send_down(z_back_low, "wide")
+    moved = exchange(grad, *steps[3])
     rest = shard_y - BY
     stretch_y = jnp.pad(stretch_low, ((0, 0), (0, rest), (0, 0))) + jnp.pad(
         stretch_high, ((0, 0), (rest, 0), (0, 0))
     )
-    moved = exchange(grad, *steps[4])
     updated = combine(*z_from, adjoint, velocity, tendency, z_low, z_high, stretch_y)
     moved, updated = after(moved, updated)
     grad = grad + moved
-    for step in steps[5:]:
+    for step in steps[4:]:
         grad = grad + exchange(grad, *step)
     return finish(updated, last_low, last_high), owner_rows(grad, turbine_owner)
 

time: 254 us -> 231 us (0.909)
  waiting for transfers between devices: 67.2 us -> 56.8 us
  local copies, waits for them, and re-layouts: 31.3 us -> 22.4 us
    ppermute x5, waiting for transfers between devices: 54 us -> 14.7 us  [exchange(): return lax.ppermute(value, axis, [(i, i ^ distance) for i in range(size)])]
    ppermute x4, waiting for transfers between devices: 13.2 us -> 42.2 us  [send_up(): return lax.ppermute(value, axis, [(i, i + 1) for i in range(size - 1)])]
    unnamed x26 -> x12, local copies, waits for them, and re-layouts: 10.9 us -> 1.64 us
    ppermute x5, starting transfers between devices: 11.4 us -> 7.99 us  [exchange(): return lax.ppermute(value, axis, [(i, i ^ distance) for i in range(size)])]
  transfers between devices with their start and end apart: 13 -> 13, of which waited for: 4 -> 3; matrix products, arithmetic and copies ran while one was open for 6% -> 4% of each run, Pallas kernels for 41% -> 48%
where the time goes in v3:
time: 231 us; the launch traced here: 230 us
  Pallas kernels  111 us (48%)
  waiting for transfers between devices  56.8 us (25%)
  starting transfers between devices  31.2 us (14%)
  local copies, waits for them, and re-layouts  22.4 us (10%)
  other arithmetic  8.47 us (4%)
    ppermute x4, waiting for transfers between devices, send_up(): return lax.ppermute(value, axis, [(i, i + 1) for i in range(size - 1)])  42.2 us
    pallas_call x1, Pallas kernels, xy_terms(): pl.pallas_call(xy_kernel, grid=(shard_z // planes,), in_specs=[whole(m) f...  34.4 us
    pallas_call x1, Pallas kernels, z_local(): pl.pallas_call(z_local_kernel, grid=(shard_y // GROUP,), in_specs=[pl.Blo...  24.4 us
    pallas_call x1, Pallas kernels, combine(): pl.pallas_call(combine_kernel, grid=(shard_y // GROUP,), in_specs=[whole(...  18.4 us
    ppermute x4, starting transfers between devices, send_up(): return lax.ppermute(value, axis, [(i, i + 1) for i in range(size - 1)])  18.1 us
    pallas_call x1, Pallas kernels, turbine_terms(): pl.pallas_call(functools.partial(turbine_kernel, count, (shard_z, shard_y...  17 us
    ppermute x5, waiting for transfers between devices, exchange(): return lax.ppermute(value, axis, [(i, i ^ distance) for i in range(size)])  14.7 us
    slice x1, local copies, waits for them, and re-layouts, on_device(): y_high = send_down(adjoint[:, :, :BY], 'narrow')  11.9 us
  transfers between devices with their start and end apart: 13, of which 3 were waited for; matrix products, arithmetic and copies ran while one was open for 4% of the time, Pallas kernels for 48%

profile of v3, /device:TPU:0, one launch (start us, length us, event | category | flops | bytes accessed | tf_op | source)
XLA Modules:
  0.0 230.3 jit_solution(17111477109838332714)
XLA Ops:
  0.6 6.4 %fusion.6 = (f32[3,16,64,256]{3,2,1,0:T(8,128)}, f32[3,16,64,256]{3,2,1,0:T(8,128)}) fusion(f32[3,64,64,256]{3,2,1,0:T(8,128)} %adjoint.2), kind=kLoop, calls=%fused_computation.26 | loop fusion | bytes 12582912 | tf_op jit(solution)/shard_map/slice | solution.py:428
  7.0 11.9 %fusion.5 = (f32[3,64,32,256]{3,2,1,0:T(8,128)}, f32[3,64,32,256]{3,2,1,0:T(8,128)}) fusion(f32[3,64,64,256]{3,2,1,0:T(8,128)} %adjoint.2), kind=kLoop, calls=%fused_computation.25 | loop fusion | bytes 25165824 | tf_op jit(solution)/shard_map/slice | solution.py:432
  18.9 4.9 %collective-permute-start.2 = (f32[3,64,32,256]{3,2,1,0:T(8,128)}, f32[3,64,32,256]{3,2,1,0:T(8,128)}, u32[]{:S(2)}, u32[]{:S(2)}) collective-permute-start(f32[3,64,32,256]{3,2,1,0:T(8,128)} %get-tuple-element.69), channel_id=1, source_target_pairs={{0,1},{1,2},{2,3},{4,5},{5,6},{6,7},{8,9},{9,10},{10,11},{12,13},{... | collective-permute-start | bytes 18874376 | tf_op jit(solution)/shard_map/ppermute | solution.py:394
  23.9 1.3 collective-permute-start.3
  25.2 4.5 %collective-permute-start.5 = (f32[3,16,64,256]{3,2,1,0:T(8,128)}, f32[3,16,64,256]{3,2,1,0:T(8,128)S(1)}, u32[]{:S(2)}, u32[]{:S(2)}) collective-permute-start(f32[3,16,64,256]{3,2,1,0:T(8,128)} %get-tuple-element.52), channel_id=1, source_target_pairs={{0,4},{4,8},{8,12},{12,16},{16,20},{20,24},{24,28},{1,5},{5,9},{9,... | collective-permute-start | bytes 9437192 | tf_op jit(solution)/shard_map/ppermute | solution.py:394
  29.6 1.3 collective-permute-start.6
  31.0 0.6 fusion.2
  31.6 0.6 fusion.3.zs
  32.2 17.0 %turbine_terms.1 = (f32[64,64,256]{2,1,0:T(8,128)}, f32[96,128]{1,0:T(8,128)}, f32[96,128]{1,0:T(8,128)}) custom-call(s32[96]{0:T(128)} %fusion.3.zs, s32[96]{0:T(128)} %get-tuple-element.66.ys, s32[96]{0:T(128)} %get-tuple-element.72.xs, f32[96]{0:T(128)} %thrust.1, f32[3,64,64,256]{3,2,1,0:T(8,128)} %adjoint.2, f32[3,64,64,256]{3,2,1,0:T(8,128)} %adjoint.2, ...), custom_call_target="tpu_custom_call" | custom-call | flops 20000 | bytes 600000 | tf_op jit(solution)/shard_map/turbine_terms/pallas_call | solution.py:172
  49.1 0.9 reduce_sum.37
  50.0 0.9 reduce_sum.36
  51.5 1.6 pad_dynamic-slice_fusion.z
  53.1 0.7 pad_dynamic-slice_fusion.1.y
  53.8 3.7 %matrices.1 = (bf16[256,512]{1,0:T(8,128)(2,1)}, bf16[128,256]{1,0:T(8,128)(2,1)}, bf16[128,128]{1,0:T(8,128)(2,1)}, bf16[64,64]{1,0:T(8,128)(2,1)}, bf16[64,64]...) custom-call(f32[256,256]{1,0:T(8,128)} %x.9, ...), custom_call_target="tpu_custom_call" | custom-call | flops 2000000 | bytes 80000 | tf_op jit(solution)/shard_map/matrices/pallas_call | solution.py:103
  57.5 24.4 %z_local.1.tendency = f32[3,64,64,256]{3,2,1,0:T(8,128)} custom-call(bf16[1024,512]{1,0:T(8,128)(2,1)} %get-tuple-element.39.matrix, f32[3,64,64,256]{3,2,1,0:T(8,128)} %adjoint.2, f32[3,64,64,256]{3,2,1,0:T(8,128)} %carrier.1), custom_call_target="tpu_custom_call" | custom-call | flops 400000000 | bytes 800000 | tf_op jit(solution)/shard_map/z_local/pallas_call | solution.py:224
  81.9 14.7 %collective-permute-done.1 = f32[2,96]{1,0:T(2,128)S(1)} collective-permute-done((f32[2,96]{1,0:T(2,128)S(1)}, f32[2,96]{1,0:T(2,128)S(1)}, u32[]{:S(2)}, u32[]{:S(2)}) %collective-permute-start.1) | collective-permute-done | bytes 800 | tf_op jit(solution)/shard_map/ppermute | solution.py:404
  96.6 34.4 %xy_terms.1 = (f32[3,64,64,256]{3,2,1,0:T(8,128)}, f32[64,32,256]{2,1,0:T(8,128)}, f32[64,32,256]{2,1,0:T(8,128)}) custom-call(bf16[256,512]{1,0:T(8,128)(2,1)} %get-tuple-element.42.matrix_x, bf16[128,256]{1,0:T(8,128)(2,1)} %get-tuple-element.43.matrix_ya, bf16[128,128]{1,0:T(8,128)(2,1)} %get-tuple-element.44.matrix_yv, ...), custom_call_target="tpu_custom_call" | custom-call | flops 400000000 | bytes 1400000 | tf_op jit(solution)/shard_map/xy_terms/pallas_call | solution.py:287
  131.0 1.3 collective-permute-start.11
  132.3 4.4 %collective-permute-start.10 = (f32[64,32,256]{2,1,0:T(8,128)}, f32[64,32,256]{2,1,0:T(8,128)}, u32[]{:S(2)}, u32[]{:S(2)}) collective-permute-start(f32[64,32,256]{2,1,0:T(8,128)} %get-tuple-element.62), channel_id=1, source_target_pairs={{0,1},{1,2},{2,3},{4,5},{5,6},{6,7},{8,9},{9,10},{10,11},{12,13},{... | collective-permute-start | bytes 6291464 | tf_op jit(solution)/shard_map/ppermute | solution.py:394
  136.7 1.6 collective-permute-start.4
  138.3 27.2 %collective-permute-done.5.halo_low = f32[3,16,64,256]{3,2,1,0:T(8,128)S(1)} collective-permute-done((f32[3,16,64,256]{3,2,1,0:T(8,128)}, f32[3,16,64,256]{3,2,1,0:T(8,128)S(1)}, u32[]{:S(2)}, u32[]{:S(2)}) %collective-permute-start.5) | collective-permute-done | bytes 3145760 | tf_op jit(solution)/shard_map/ppermute | solution.py:394
  165.5 1.6 copy-done.2
  167.1 8.8 %z_back.1 = (f32[16,64,256]{2,1,0:T(8,128)S(1)}, f32[16,64,256]{2,1,0:T(8,128)}) custom-call(bf16[256,256]{1,0:T(8,128)(2,1)S(1)} %copy-done, bf16[256,256]{1,0:T(8,128)(2,1)S(1)} %copy-done.1, f32[3,64,64,256]{3,2,1,0:T(8,128)} %carrier.1, f32[3,64,64,256]{3,2,1,0:T(8,128)} %carrier.1, f32[3,16,64,256]{3,2,1,0:T(8,128)} %copy-done.2, ...), custom_call_target="tpu_custom_call" | custom-call | flops 60000000 | bytes 400000 | tf_op jit(solution)/shard_map/z_back/pallas_call | solution.py:320
  175.9 4.3 %collective-permute-start.7 = (f32[16,64,256]{2,1,0:T(8,128)}, f32[16,64,256]{2,1,0:T(8,128)S(1)}, u32[]{:S(2)}, u32[]{:S(2)}) collective-permute-start(f32[16,64,256]{2,1,0:T(8,128)} %get-tuple-element.56), channel_id=1, source_target_pairs={{0,4},{4,8},{8,12},{12,16},{16,20},{20,24},{24,28},{1,5},{5,9},{9,... | collective-permute-start | bytes 3145736 | tf_op jit(solution)/shard_map/ppermute | solution.py:394
  180.3 1.3 collective-permute-start.8
  181.8 3.2 %collective-permute-start.9 = (f32[2,96]{1,0:T(2,128)S(1)}, f32[2,96]{1,0:T(2,128)S(1)}, u32[]{:S(2)}, u32[]{:S(2)}) collective-permute-start(f32[2,96]{1,0:T(2,128)S(1)} %add.55), channel_id=1, source_target_pairs={{0,8},{4,12},{8,0},{12,4},{16,24},{20,28},{24,16},{28,20},{1,9},{5... | collective-permute-start | bytes 2312 | tf_op jit(solution)/shard_map/ppermute | solution.py:404
  185.0 4.6 %pad_add_fusion.stretch_y = f32[64,64,256]{2,1,0:T(8,128)} fusion(f32[64,32,256]{2,1,0:T(8,128)} %collective-permute-done.11, f32[64,32,256]{2,1,0:T(8,128)} %collective-permute-done.10), kind=kLoop, calls=%fused_computation | loop fusion | flops 1048576 | bytes 8388608 | tf_op jit(solution)/shard_map/add | solution.py:462
  189.6 18.4 %combine.1.updated = f32[3,64,64,256]{3,2,1,0:T(8,128)} custom-call(bf16[256,256]{1,0:T(8,128)(2,1)} %get-tuple-element.59.from_low, bf16[256,256]{1,0:T(8,128)(2,1)} %get-tuple-element.60.from_high, f32[3,64,64,256]{3,2,1,0:T(8,128)} %adjoint.2, f32[3,64,64,256]{3,2,1,0:T(8,128)} %carrier.1, f32[3,64,64,256]{3,2,1,0:T(8,128)} %get-tuple-element.61.tendency, ...), custom_call_target="tpu_custom_call" | custom-call | flops 60000000 | bytes 1000000 | tf_op jit(solution)/shard_map/combine/pallas_call | solution.py:356
  208.1 2.7 %collective-permute-start.12 = (f32[2,96]{1,0:T(2,128)S(1)}, f32[2,96]{1,0:T(2,128)S(1)}, u32[]{:S(2)}, u32[]{:S(2)}) collective-permute-start(f32[2,96]{1,0:T(2,128)S(1)} %add.58), channel_id=1, source_target_pairs={{0,16},{4,20},{8,24},{12,28},{16,0},{20,4},{24,8},{28,12},{1,17},{... | collective-permute-start | bytes 2312 | tf_op jit(solution)/shard_map/ppermute | solution.py:404
  210.7 15.0 %collective-permute-done.7.back_low = f32[16,64,256]{2,1,0:T(8,128)S(1)} collective-permute-done((f32[16,64,256]{2,1,0:T(8,128)}, f32[16,64,256]{2,1,0:T(8,128)S(1)}, u32[]{:S(2)}, u32[]{:S(2)}) %collective-permute-start.7) | collective-permute-done | bytes 1048608 | tf_op jit(solution)/shard_map/ppermute | solution.py:394
  225.7 4.0 %finish.1 = f32[3,64,64,256]{3,2,1,0:T(8,128)} custom-call(f32[16,64,256]{2,1,0:T(8,128)S(1)} %collective-permute-done.7.back_low, f32[16,64,256]{2,1,0:T(8,128)S(1)} %collective-permute-done.8.back_high, f32[3,64,64,256]{3,2,1,0:T(8,128)} %combine.1.updated), custom_call_target="tpu_custom_call", output_to_operand_aliasing={{}: (2, {})} | custom-call | flops 20000 | bytes 120000 | tf_op jit(solution)/shard_map/finish/pallas_call | solution.py:379
  229.7 0.7 select_reduce_fusion
  (33 shorter events, 0.9 us)
Async XLA Ops:
  7.0 23.9 %copy-start.4 = (s32[96,128]{1,0:T(8,128)S(1)}, s32[96,128]{1,0:T(8,128)}, u32[]{:S(2)}) copy-start(s32[96,128]{1,0:T(8,128)} %param.14) | copy-start | bytes 147460
  18.9 77.7 %collective-permute-start.2 = (f32[3,64,32,256]{3,2,1,0:T(8,128)}, f32[3,64,32,256]{3,2,1,0:T(8,128)}, u32[]{:S(2)}, u32[]{:S(2)}) collective-permute-start(f32[3,64,32,256]{3,2,1,0:T(8,128)} %get-tuple-element.69), channel_id=1, source_target_pairs={{0,1},{1,2},{2,3},{4,5},{5,6},{6,7},{8,9},{9,10},{10,11},{12,13},{... | collective-permute-start | bytes 18874376 | tf_op jit(solution)/shard_map/ppermute | solution.py:394
  23.9 72.7 %collective-permute-start.3 = (f32[3,64,32,256]{3,2,1,0:T(8,128)}, f32[3,64,32,256]{3,2,1,0:T(8,128)}, u32[]{:S(2)}, u32[]{:S(2)}) collective-permute-start(f32[3,64,32,256]{3,2,1,0:T(8,128)} %get-tuple-element.68), channel_id=1, source_target_pairs={{1,0},{2,1},{3,2},{5,4},{6,5},{7,6},{9,8},{10,9},{11,10},{13,12},{... | collective-permute-start | bytes 18874376 | tf_op jit(solution)/shard_map/ppermute | solution.py:399
  25.2 140.3 %collective-permute-start.5 = (f32[3,16,64,256]{3,2,1,0:T(8,128)}, f32[3,16,64,256]{3,2,1,0:T(8,128)S(1)}, u32[]{:S(2)}, u32[]{:S(2)}) collective-permute-start(f32[3,16,64,256]{3,2,1,0:T(8,128)} %get-tuple-element.52), channel_id=1, source_target_pairs={{0,4},{4,8},{8,12},{12,16},{16,20},{20,24},{24,28},{1,5},{5,9},{9,... | collective-permute-start | bytes 9437192 | tf_op jit(solution)/shard_map/ppermute | solution.py:394
  29.6 135.8 %collective-permute-start.6 = (f32[3,16,64,256]{3,2,1,0:T(8,128)}, f32[3,16,64,256]{3,2,1,0:T(8,128)}, u32[]{:S(2)}, u32[]{:S(2)}) collective-permute-start(f32[3,16,64,256]{3,2,1,0:T(8,128)} %get-tuple-element.53), channel_id=1, source_target_pairs={{4,0},{8,4},{12,8},{16,12},{20,16},{24,20},{28,24},{5,1},{9,5},{13... | collective-permute-start | bytes 9437192 | tf_op jit(solution)/shard_map/ppermute | solution.py:399
  32.2 20.9 %copy-start.3 = (f32[256,256]{1,0:T(8,128)S(1)}, f32[256,256]{1,0:T(8,128)}, u32[]{:S(2)}) copy-start(f32[256,256]{1,0:T(8,128)} %param.12) | copy-start | bytes 786436
  51.0 30.9 %collective-permute-start = (f32[2,96]{1,0:T(2,128)S(1)}, f32[2,96]{1,0:T(2,128)S(1)}, u32[]{:S(2)}, u32[]{:S(2)}) collective-permute-start(f32[2,96]{1,0:T(2,128)S(1)} %maximum_multiply_fusion), channel_id=1, source_target_pairs={{0,1},{1,0},{2,3},{3,2},{4,5},{5,4},{6,7},{7,6},{8,9},{9,8},{10,11... | collective-permute-start | bytes 2312 | tf_op jit(solution)/shard_map/ppermute | solution.py:404
  81.8 14.7 %collective-permute-start.1 = (f32[2,96]{1,0:T(2,128)S(1)}, f32[2,96]{1,0:T(2,128)S(1)}, u32[]{:S(2)}, u32[]{:S(2)}) collective-permute-start(f32[2,96]{1,0:T(2,128)S(1)} %fusion.4), channel_id=1, source_target_pairs={{0,2},{1,3},{2,0},{3,1},{4,6},{5,7},{6,4},{7,5},{8,10},{9,11},{10,... | collective-permute-start | bytes 2312 | tf_op jit(solution)/shard_map/ppermute | solution.py:404
  96.6 70.5 %copy-start = (bf16[256,256]{1,0:T(8,128)(2,1)S(1)}, bf16[256,256]{1,0:T(8,128)(2,1)}, u32[]{:S(2)}) copy-start(bf16[256,256]{1,0:T(8,128)(2,1)} %get-tuple-element.34.edge_low) | copy-start | bytes 393220
  96.6 70.5 %copy-start.1 = (bf16[256,256]{1,0:T(8,128)(2,1)S(1)}, bf16[256,256]{1,0:T(8,128)(2,1)}, u32[]{:S(2)}) copy-start(bf16[256,256]{1,0:T(8,128)(2,1)} %get-tuple-element.35.edge_high) | copy-start | bytes 393220
  131.0 54.0 %collective-permute-start.11 = (f32[64,32,256]{2,1,0:T(8,128)}, f32[64,32,256]{2,1,0:T(8,128)}, u32[]{:S(2)}, u32[]{:S(2)}) collective-permute-start(f32[64,32,256]{2,1,0:T(8,128)} %get-tuple-element.63), channel_id=1, source_target_pairs={{1,0},{2,1},{3,2},{5,4},{6,5},{7,6},{9,8},{10,9},{11,10},{13,12},{... | collective-permute-start | bytes 6291464 | tf_op jit(solution)/shard_map/ppermute | solution.py:399
  132.3 52.7 %collective-permute-start.10 = (f32[64,32,256]{2,1,0:T(8,128)}, f32[64,32,256]{2,1,0:T(8,128)}, u32[]{:S(2)}, u32[]{:S(2)}) collective-permute-start(f32[64,32,256]{2,1,0:T(8,128)} %get-tuple-element.62), channel_id=1, source_target_pairs={{0,1},{1,2},{2,3},{4,5},{5,6},{6,7},{8,9},{9,10},{10,11},{12,13},{... | collective-permute-start | bytes 6291464 | tf_op jit(solution)/shard_map/ppermute | solution.py:394
  136.7 28.8 %collective-permute-start.4 = (f32[2,96]{1,0:T(2,128)S(1)}, f32[2,96]{1,0:T(2,128)S(1)}, u32[]{:S(2)}, u32[]{:S(2)}) collective-permute-start(f32[2,96]{1,0:T(2,128)S(1)} %fusion.7), channel_id=1, source_target_pairs={{0,4},{4,0},{8,12},{12,8},{16,20},{20,16},{24,28},{28,24},{1,5},{5... | collective-permute-start | bytes 2312 | tf_op jit(solution)/shard_map/ppermute | solution.py:404
  165.5 1.6 copy-start.2
  167.1 14.5 %copy-start.5 = (s32[96]{0:T(128)S(1)}, s32[96]{0:T(128)}, u32[]{:S(2)}) copy-start(s32[96]{0:T(128)} %param.15) | copy-start | bytes 1156
  175.9 49.8 %collective-permute-start.7 = (f32[16,64,256]{2,1,0:T(8,128)}, f32[16,64,256]{2,1,0:T(8,128)S(1)}, u32[]{:S(2)}, u32[]{:S(2)}) collective-permute-start(f32[16,64,256]{2,1,0:T(8,128)} %get-tuple-element.56), channel_id=1, source_target_pairs={{0,4},{4,8},{8,12},{12,16},{16,20},{20,24},{24,28},{1,5},{5,9},{9,... | collective-permute-start | bytes 3145736 | tf_op jit(solution)/shard_map/ppermute | solution.py:394
  180.3 45.4 %collective-permute-start.8 = (f32[16,64,256]{2,1,0:T(8,128)S(1)}, f32[16,64,256]{2,1,0:T(8,128)S(1)}, u32[]{:S(2)}, u32[]{:S(2)}) collective-permute-start(f32[16,64,256]{2,1,0:T(8,128)S(1)} %get-tuple-element.57), channel_id=1, source_target_pairs={{4,0},{8,4},{12,8},{16,12},{20,16},{24,20},{28,24},{5,1},{9,5},{13... | collective-permute-start | bytes 3145736 | tf_op jit(solution)/shard_map/ppermute | solution.py:399
  181.8 26.3 %collective-permute-start.9 = (f32[2,96]{1,0:T(2,128)S(1)}, f32[2,96]{1,0:T(2,128)S(1)}, u32[]{:S(2)}, u32[]{:S(2)}) collective-permute-start(f32[2,96]{1,0:T(2,128)S(1)} %add.55), channel_id=1, source_target_pairs={{0,8},{4,12},{8,0},{12,4},{16,24},{20,28},{24,16},{28,20},{1,9},{5... | collective-permute-start | bytes 2312 | tf_op jit(solution)/shard_map/ppermute | solution.py:404
  208.1 21.6 %collective-permute-start.12 = (f32[2,96]{1,0:T(2,128)S(1)}, f32[2,96]{1,0:T(2,128)S(1)}, u32[]{:S(2)}, u32[]{:S(2)}) collective-permute-start(f32[2,96]{1,0:T(2,128)S(1)} %add.58), channel_id=1, source_target_pairs={{0,16},{4,20},{8,24},{12,28},{16,0},{20,4},{24,8},{28,12},{1,17},{... | collective-permute-start | bytes 2312 | tf_op jit(solution)/shard_map/ppermute | solution.py:404

commit v4 on v3

--- a/solution.py
+++ b/solution.py
@@ -297,29 +297,32 @@
 
 
 def z_back_kernel(edge_low, edge_high, vel_low, vel_high, halo_low, halo_high, back_low, back_high):
-    _, band, group, extent = vel_low.shape
-    rows = band * group
+    _, band, lines, extent = vel_low.shape
+    rows = band * GROUP
     for edge, vel, halo, back in (
         (edge_low, vel_low, halo_low, back_low),
         (edge_high, vel_high, halo_high, back_high),
     ):
-        total = jnp.zeros((rows, extent), jnp.float32)
-        for c in range(3):
-            value = vel[c].reshape(rows, extent)
-            total += halo[c].reshape(rows, extent) * apply_stacked(edge[...], value)
-        back[...] = total.reshape(band, group, extent)
+        for first in range(0, lines, GROUP):
+            at = slice(first, first + GROUP)
+            total = jnp.zeros((rows, extent), jnp.float32)
+            for c in range(3):
+                value = vel[c, :, at].reshape(rows, extent)
+                total += halo[c, :, at].reshape(rows, extent) * apply_stacked(edge[...], value)
+            back[:, at] = total.reshape(band, GROUP, extent)
 
 
 def z_back(edge_low, edge_high, velocity, halo_low, halo_high):
     _, shard_z, shard_y, extent = velocity.shape
     last = shard_z // BAND - 1
+    lines = 2 * GROUP
     whole = lambda m: pl.BlockSpec(m.shape, lambda i: (0, 0))
-    edge = lambda at: pl.BlockSpec((3, BAND, GROUP, extent), lambda i: (0, at, i, 0))
-    back = pl.BlockSpec((BAND, GROUP, extent), lambda i: (0, i, 0))
+    edge = lambda at: pl.BlockSpec((3, BAND, lines, extent), lambda i: (0, at, i, 0))
+    back = pl.BlockSpec((BAND, lines, extent), lambda i: (0, i, 0))
     shape = jax.ShapeDtypeStruct((BAND, shard_y, extent), jnp.float32)
     return pl.pallas_call(
         z_back_kernel,
-        grid=(shard_y // GROUP,),
+        grid=(shard_y // lines,),
         in_specs=[whole(edge_low), whole(edge_high), edge(0), edge(last), edge(0), edge(0)],
         out_specs=[back, back],
         out_shape=[shape, shape],
@@ -389,6 +392,37 @@
     )(back_low, back_high, updated)
 
 
+def edges_kernel(adjoint, top, bottom, left, right, sems):
+    _, shard_z, shard_y, _ = adjoint.shape
+    copies = [
+        pltpu.make_async_copy(adjoint.at[:, pl.ds(shard_z - BAND, BAND)], top, sems.at[0]),
+        pltpu.make_async_copy(adjoint.at[:, pl.ds(0, BAND)], bottom, sems.at[1]),
+        pltpu.make_async_copy(adjoint.at[:, :, pl.ds(shard_y - BY, BY)], left, sems.at[2]),
+        pltpu.make_async_copy(adjoint.at[:, :, pl.ds(0, BY)], right, sems.at[3]),
+    ]
+    for copy in copies:
+        copy.start()
+    for copy in copies:
+        copy.wait()
+
+
+def edges(adjoint):
+    parts, shard_z, shard_y, extent = adjoint.shape
+    planes = jax.ShapeDtypeStruct((parts, BAND, shard_y, extent), jnp.float32)
+    lines = jax.ShapeDtypeStruct((parts, shard_z, BY, extent), jnp.float32)
+    hbm = pl.BlockSpec(memory_space=pl.ANY)
+    return pl.pallas_call(
+        edges_kernel,
+        in_specs=[hbm],
+        out_specs=[hbm] * 4,
+        out_shape=[planes, planes, lines, lines],
+        scratch_shapes=[pltpu.SemaphoreType.DMA((4,))],
+        compiler_params=params(),
+        cost_estimate=cost(1e6, 4e7),
+        name="edges",
+    )(adjoint)
+
+
 def send_up(value, axis):
     size = lax.axis_size(axis)
     return lax.ppermute(value, axis, [(i, i + 1) for i in range(size - 1)])
@@ -425,11 +459,11 @@
     adjoint, velocity, deriv_x, deriv_y, deriv_z, rotor_blocks, turbine_owner, disk_weight, thrust
 ):
     _, shard_z, shard_y, extent = adjoint.shape
-    top, bottom, adjoint = after(adjoint[:, shard_z - BAND :], adjoint[:, :BAND], adjoint)
+    top, bottom, left, right = edges(adjoint)
     z_low = send_up(top, "wide")
     z_high = send_down(bottom, "wide")
-    y_low = send_up(adjoint[:, :, shard_y - BY :], "narrow")
-    y_high = send_down(adjoint[:, :, :BY], "narrow")
+    y_low = send_up(left, "narrow")
+    y_high = send_down(right, "narrow")
 
     steps = [("narrow", 2**k) for k in range(8) if 2**k < lax.axis_size("narrow")]
     steps += [("wide", 2**k) for k in range(8) if 2**k < lax.axis_size("wide")]

time: 231 us -> 784 us (3.39)
  Pallas kernels: 111 us -> 682 us
  local copies, waits for them, and re-layouts: 22.4 us -> 4.08 us
    pallas_call x1 -> x2, Pallas kernels: 8.81 us -> 580 us  [the longest x1 573 us: edges(): pl.pallas_call(edges_kernel, in_specs=[hbm], out_specs=[hbm] * 4, out_sha...]
    slice x2 -> x0, local copies, waits for them, and re-layouts: 18.3 us -> none  [the longest x1 11.9 us: on_device(): y_high = send_down(adjoint[:, :, :BY], 'narrow')]
  transfers between devices with their start and end apart: 13 -> 13, of which waited for: 3 -> 3; matrix products, arithmetic and copies ran while one was open for 4% -> 1% of each run, Pallas kernels for 48% -> 14%
where the time goes in v4:
time: 784 us; the launch traced here: 783 us
  Pallas kernels  682 us (87%)
  waiting for transfers between devices  56.5 us (7%)
  starting transfers between devices  31.3 us (4%)
  other arithmetic  8.43 us (1%)
    pallas_call x1, Pallas kernels, edges(): pl.pallas_call(edges_kernel, in_specs=[hbm], out_specs=[hbm] * 4, out_sha...  573 us
    ppermute x4, waiting for transfers between devices, send_up(): return lax.ppermute(value, axis, [(i, i + 1) for i in range(size - 1)])  42.2 us
    pallas_call x1, Pallas kernels, xy_terms(): pl.pallas_call(xy_kernel, grid=(shard_z // planes,), in_specs=[whole(m) f...  34.4 us
    pallas_call x1, Pallas kernels, z_local(): pl.pallas_call(z_local_kernel, grid=(shard_y // GROUP,), in_specs=[pl.Blo...  24.4 us
    pallas_call x1, Pallas kernels, combine(): pl.pallas_call(combine_kernel, grid=(shard_y // GROUP,), in_specs=[whole(...  18.4 us
    ppermute x4, starting transfers between devices, send_up(): return lax.ppermute(value, axis, [(i, i + 1) for i in range(size - 1)])  18.1 us
    pallas_call x1, Pallas kernels, turbine_terms(): pl.pallas_call(functools.partial(turbine_kernel, count, (shard_z, shard_y...  17.3 us
  transfers between devices with their start and end apart: 13, of which 3 were waited for; matrix products, arithmetic and copies ran while one was open for 1% of the time, Pallas kernels for 14%

profile of v4, /device:TPU:0, one launch (start us, length us, event | category | flops | bytes accessed | tf_op | source)
XLA Modules:
  0.0 783.2 jit_solution(12436032330054820330)
XLA Ops:
  0.6 572.9 %edges.1 = (f32[3,16,64,256]{3,2,1,0:T(8,128)}, f32[3,16,64,256]{3,2,1,0:T(8,128)}, f32[3,64,32,256]{3,2,1,0:T(8,128)}, f32[3,64,32,256]{3,2,1,0:T(8,128)}) custom-call(f32[3,64,64,256]{3,2,1,0:T(8,128)} %adjoint.7), custom_call_target="tpu_custom_call" | custom-call | flops 20000 | bytes 800000 | tf_op jit(solution)/shard_map/edges/pallas_call | solution.py:414
  573.5 5.0 collective-permute-start.2
  578.5 1.3 collective-permute-start.3
  579.8 4.5 collective-permute-start.5
  584.3 1.3 collective-permute-start.6
  585.7 0.5 fusion.2
  586.2 0.5 fusion.3.zs
  586.8 17.3 %turbine_terms.1 = (f32[64,64,256]{2,1,0:T(8,128)}, f32[96,128]{1,0:T(8,128)}, f32[96,128]{1,0:T(8,128)}) custom-call(s32[96]{0:T(128)} %fusion.3.zs, s32[96]{0:T(128)} %get-tuple-element.68.ys, s32[96]{0:T(128)} %get-tuple-element.70.xs, f32[96]{0:T(128)} %thrust.1, f32[3,64,64,256]{3,2,1,0:T(8,128)} %adjoint.7, f32[3,64,64,256]{3,2,1,0:T(8,128)} %adjoint.7, ...), custom_call_target="tpu_custom_call" | custom-call | flops 20000 | bytes 600000 | tf_op jit(solution)/shard_map/turbine_terms/pallas_call | solution.py:172
  604.0 0.9 reduce_sum.37
  605.0 0.9 reduce_sum.36
  606.0 1.6 pad_dynamic-slice_fusion.z
  607.6 0.7 pad_dynamic-slice_fusion.1.y
  608.3 3.6 matrices.1
  611.9 24.4 %z_local.1.tendency = f32[3,64,64,256]{3,2,1,0:T(8,128)} custom-call(bf16[1024,512]{1,0:T(8,128)(2,1)} %get-tuple-element.39.matrix, f32[3,64,64,256]{3,2,1,0:T(8,128)} %adjoint.7, f32[3,64,64,256]{3,2,1,0:T(8,128)} %carrier.1), custom_call_target="tpu_custom_call" | custom-call | flops 400000000 | bytes 800000 | tf_op jit(solution)/shard_map/z_local/pallas_call | solution.py:224
  636.3 0.6 collective-permute-start.1
  636.9 14.3 %collective-permute-done.1 = f32[2,96]{1,0:T(2,128)S(1)} collective-permute-done((f32[2,96]{1,0:T(2,128)S(1)}, f32[2,96]{1,0:T(2,128)S(1)}, u32[]{:S(2)}, u32[]{:S(2)}) %collective-permute-start.1) | collective-permute-done | bytes 800 | tf_op jit(solution)/shard_map/ppermute | solution.py:438
  651.2 34.4 %xy_terms.1 = (f32[3,64,64,256]{3,2,1,0:T(8,128)}, f32[64,32,256]{2,1,0:T(8,128)}, f32[64,32,256]{2,1,0:T(8,128)}) custom-call(bf16[256,512]{1,0:T(8,128)(2,1)} %get-tuple-element.44.matrix_x, bf16[128,256]{1,0:T(8,128)(2,1)} %get-tuple-element.45.matrix_ya, bf16[128,128]{1,0:T(8,128)(2,1)} %get-tuple-element.46.matrix_yv, ...), custom_call_target="tpu_custom_call" | custom-call | flops 400000000 | bytes 1400000 | tf_op jit(solution)/shard_map/xy_terms/pallas_call | solution.py:287
  685.6 1.3 collective-permute-start.11
  686.9 4.4 collective-permute-start.10
  691.3 1.6 collective-permute-start.4
  692.9 27.2 %collective-permute-done.5.halo_low = f32[3,16,64,256]{3,2,1,0:T(8,128)S(1)} collective-permute-done((f32[3,16,64,256]{3,2,1,0:T(8,128)}, f32[3,16,64,256]{3,2,1,0:T(8,128)S(1)}, u32[]{:S(2)}, u32[]{:S(2)}) %collective-permute-start.5) | collective-permute-done | bytes 3145760 | tf_op jit(solution)/shard_map/ppermute | solution.py:428
  720.1 1.6 copy-done.2
  721.7 7.1 z_back.1
  728.8 4.3 collective-permute-start.7
  733.1 1.3 collective-permute-start.8
  734.7 3.2 collective-permute-start.9
  737.8 4.7 pad_add_fusion.stretch_y
  742.5 18.4 %combine.1.updated = f32[3,64,64,256]{3,2,1,0:T(8,128)} custom-call(bf16[256,256]{1,0:T(8,128)(2,1)} %get-tuple-element.61.from_low, bf16[256,256]{1,0:T(8,128)(2,1)} %get-tuple-element.62.from_high, f32[3,64,64,256]{3,2,1,0:T(8,128)} %adjoint.7, f32[3,64,64,256]{3,2,1,0:T(8,128)} %carrier.1, f32[3,64,64,256]{3,2,1,0:T(8,128)} %get-tuple-element.63.tendency, ...), custom_call_target="tpu_custom_call" | custom-call | flops 60000000 | bytes 1000000 | tf_op jit(solution)/shard_map/combine/pallas_call | solution.py:359
  761.0 2.6 collective-permute-start.12
  763.6 14.9 %collective-permute-done.7.back_low = f32[16,64,256]{2,1,0:T(8,128)S(1)} collective-permute-done((f32[16,64,256]{2,1,0:T(8,128)}, f32[16,64,256]{2,1,0:T(8,128)S(1)}, u32[]{:S(2)}, u32[]{:S(2)}) %collective-permute-start.7) | collective-permute-done | bytes 1048608 | tf_op jit(solution)/shard_map/ppermute | solution.py:428
  778.6 4.0 finish.1
  782.6 0.7 select_reduce_fusion
  (32 shorter events, 0.5 us)
Async XLA Ops:
  0.6 584.9 %copy-start.4 = (s32[96,128]{1,0:T(8,128)S(1)}, s32[96,128]{1,0:T(8,128)}, u32[]{:S(2)}) copy-start(s32[96,128]{1,0:T(8,128)} %param.14) | copy-start | bytes 147460
  573.5 77.7 %collective-permute-start.2 = (f32[3,64,32,256]{3,2,1,0:T(8,128)}, f32[3,64,32,256]{3,2,1,0:T(8,128)}, u32[]{:S(2)}, u32[]{:S(2)}) collective-permute-start(f32[3,64,32,256]{3,2,1,0:T(8,128)} %get-tuple-element.41), channel_id=1, source_target_pairs={{0,1},{1,2},{2,3},{4,5},{5,6},{6,7},{8,9},{9,10},{10,11},{12,13},{... | collective-permute-start | bytes 18874376 | tf_op jit(solution)/shard_map/ppermute | solution.py:428
  578.5 72.7 %collective-permute-start.3 = (f32[3,64,32,256]{3,2,1,0:T(8,128)}, f32[3,64,32,256]{3,2,1,0:T(8,128)}, u32[]{:S(2)}, u32[]{:S(2)}) collective-permute-start(f32[3,64,32,256]{3,2,1,0:T(8,128)} %get-tuple-element.42), channel_id=1, source_target_pairs={{1,0},{2,1},{3,2},{5,4},{6,5},{7,6},{9,8},{10,9},{11,10},{13,12},{... | collective-permute-start | bytes 18874376 | tf_op jit(solution)/shard_map/ppermute | solution.py:433
  579.8 140.3 %collective-permute-start.5 = (f32[3,16,64,256]{3,2,1,0:T(8,128)}, f32[3,16,64,256]{3,2,1,0:T(8,128)S(1)}, u32[]{:S(2)}, u32[]{:S(2)}) collective-permute-start(f32[3,16,64,256]{3,2,1,0:T(8,128)} %get-tuple-element.54), channel_id=1, source_target_pairs={{0,4},{4,8},{8,12},{12,16},{16,20},{20,24},{24,28},{1,5},{5,9},{9,... | collective-permute-start | bytes 9437192 | tf_op jit(solution)/shard_map/ppermute | solution.py:428
  584.3 135.8 %collective-permute-start.6 = (f32[3,16,64,256]{3,2,1,0:T(8,128)}, f32[3,16,64,256]{3,2,1,0:T(8,128)}, u32[]{:S(2)}, u32[]{:S(2)}) collective-permute-start(f32[3,16,64,256]{3,2,1,0:T(8,128)} %get-tuple-element.55), channel_id=1, source_target_pairs={{4,0},{8,4},{12,8},{16,12},{20,16},{24,20},{28,24},{5,1},{9,5},{13... | collective-permute-start | bytes 9437192 | tf_op jit(solution)/shard_map/ppermute | solution.py:433
  586.8 20.8 %copy-start.3 = (f32[256,256]{1,0:T(8,128)S(1)}, f32[256,256]{1,0:T(8,128)}, u32[]{:S(2)}) copy-start(f32[256,256]{1,0:T(8,128)} %param.12) | copy-start | bytes 786436
  605.9 30.4 %collective-permute-start = (f32[2,96]{1,0:T(2,128)S(1)}, f32[2,96]{1,0:T(2,128)S(1)}, u32[]{:S(2)}, u32[]{:S(2)}) collective-permute-start(f32[2,96]{1,0:T(2,128)S(1)} %maximum_multiply_fusion), channel_id=1, source_target_pairs={{0,1},{1,0},{2,3},{3,2},{4,5},{5,4},{6,7},{7,6},{8,9},{9,8},{10,11... | collective-permute-start | bytes 2312 | tf_op jit(solution)/shard_map/ppermute | solution.py:438
  636.3 14.9 %collective-permute-start.1 = (f32[2,96]{1,0:T(2,128)S(1)}, f32[2,96]{1,0:T(2,128)S(1)}, u32[]{:S(2)}, u32[]{:S(2)}) collective-permute-start(f32[2,96]{1,0:T(2,128)S(1)} %fusion.4), channel_id=1, source_target_pairs={{0,2},{1,3},{2,0},{3,1},{4,6},{5,7},{6,4},{7,5},{8,10},{9,11},{10,... | collective-permute-start | bytes 2312 | tf_op jit(solution)/shard_map/ppermute | solution.py:438
  651.2 70.5 %copy-start = (bf16[256,256]{1,0:T(8,128)(2,1)S(1)}, bf16[256,256]{1,0:T(8,128)(2,1)}, u32[]{:S(2)}) copy-start(bf16[256,256]{1,0:T(8,128)(2,1)} %get-tuple-element.35.edge_low) | copy-start | bytes 393220
  651.2 70.5 %copy-start.1 = (bf16[256,256]{1,0:T(8,128)(2,1)S(1)}, bf16[256,256]{1,0:T(8,128)(2,1)}, u32[]{:S(2)}) copy-start(bf16[256,256]{1,0:T(8,128)(2,1)} %get-tuple-element.36.edge_high) | copy-start | bytes 393220
  685.6 52.2 %collective-permute-start.11 = (f32[64,32,256]{2,1,0:T(8,128)}, f32[64,32,256]{2,1,0:T(8,128)}, u32[]{:S(2)}, u32[]{:S(2)}) collective-permute-start(f32[64,32,256]{2,1,0:T(8,128)} %get-tuple-element.65), channel_id=1, source_target_pairs={{1,0},{2,1},{3,2},{5,4},{6,5},{7,6},{9,8},{10,9},{11,10},{13,12},{... | collective-permute-start | bytes 6291464 | tf_op jit(solution)/shard_map/ppermute | solution.py:433
  686.9 50.9 %collective-permute-start.10 = (f32[64,32,256]{2,1,0:T(8,128)}, f32[64,32,256]{2,1,0:T(8,128)}, u32[]{:S(2)}, u32[]{:S(2)}) collective-permute-start(f32[64,32,256]{2,1,0:T(8,128)} %get-tuple-element.64), channel_id=1, source_target_pairs={{0,1},{1,2},{2,3},{4,5},{5,6},{6,7},{8,9},{9,10},{10,11},{12,13},{... | collective-permute-start | bytes 6291464 | tf_op jit(solution)/shard_map/ppermute | solution.py:428
  691.3 28.8 %collective-permute-start.4 = (f32[2,96]{1,0:T(2,128)S(1)}, f32[2,96]{1,0:T(2,128)S(1)}, u32[]{:S(2)}, u32[]{:S(2)}) collective-permute-start(f32[2,96]{1,0:T(2,128)S(1)} %fusion.5), channel_id=1, source_target_pairs={{0,4},{4,0},{8,12},{12,8},{16,20},{20,16},{24,28},{28,24},{1,5},{5... | collective-permute-start | bytes 2312 | tf_op jit(solution)/shard_map/ppermute | solution.py:438
  720.1 1.6 copy-start.2
  721.7 12.7 %copy-start.5 = (s32[96]{0:T(128)S(1)}, s32[96]{0:T(128)}, u32[]{:S(2)}) copy-start(s32[96]{0:T(128)} %param.15) | copy-start | bytes 1156
  728.8 49.8 %collective-permute-start.7 = (f32[16,64,256]{2,1,0:T(8,128)}, f32[16,64,256]{2,1,0:T(8,128)S(1)}, u32[]{:S(2)}, u32[]{:S(2)}) collective-permute-start(f32[16,64,256]{2,1,0:T(8,128)} %get-tuple-element.58), channel_id=1, source_target_pairs={{0,4},{4,8},{8,12},{12,16},{16,20},{20,24},{24,28},{1,5},{5,9},{9,... | collective-permute-start | bytes 3145736 | tf_op jit(solution)/shard_map/ppermute | solution.py:428
  733.1 45.4 %collective-permute-start.8 = (f32[16,64,256]{2,1,0:T(8,128)S(1)}, f32[16,64,256]{2,1,0:T(8,128)S(1)}, u32[]{:S(2)}, u32[]{:S(2)}) collective-permute-start(f32[16,64,256]{2,1,0:T(8,128)S(1)} %get-tuple-element.59), channel_id=1, source_target_pairs={{4,0},{8,4},{12,8},{16,12},{20,16},{24,20},{28,24},{5,1},{9,5},{13... | collective-permute-start | bytes 3145736 | tf_op jit(solution)/shard_map/ppermute | solution.py:433
  734.7 26.3 %collective-permute-start.9 = (f32[2,96]{1,0:T(2,128)S(1)}, f32[2,96]{1,0:T(2,128)S(1)}, u32[]{:S(2)}, u32[]{:S(2)}) collective-permute-start(f32[2,96]{1,0:T(2,128)S(1)} %add.55), channel_id=1, source_target_pairs={{0,8},{4,12},{8,0},{12,4},{16,24},{20,28},{24,16},{28,20},{1,9},{5... | collective-permute-start | bytes 2312 | tf_op jit(solution)/shard_map/ppermute | solution.py:438
  761.0 21.6 %collective-permute-start.12 = (f32[2,96]{1,0:T(2,128)S(1)}, f32[2,96]{1,0:T(2,128)S(1)}, u32[]{:S(2)}, u32[]{:S(2)}) collective-permute-start(f32[2,96]{1,0:T(2,128)S(1)} %add.58), channel_id=1, source_target_pairs={{0,16},{4,20},{8,24},{12,28},{16,0},{20,4},{24,8},{28,12},{1,17},{... | collective-permute-start | bytes 2312 | tf_op jit(solution)/shard_map/ppermute | solution.py:438

commit v5 on v4

--- a/solution.py
+++ b/solution.py
@@ -392,31 +392,41 @@
     )(back_low, back_high, updated)
 
 
-def edges_kernel(adjoint, top, bottom, left, right, sems):
-    _, shard_z, shard_y, _ = adjoint.shape
-    copies = [
-        pltpu.make_async_copy(adjoint.at[:, pl.ds(shard_z - BAND, BAND)], top, sems.at[0]),
-        pltpu.make_async_copy(adjoint.at[:, pl.ds(0, BAND)], bottom, sems.at[1]),
-        pltpu.make_async_copy(adjoint.at[:, :, pl.ds(shard_y - BY, BY)], left, sems.at[2]),
-        pltpu.make_async_copy(adjoint.at[:, :, pl.ds(0, BY)], right, sems.at[3]),
-    ]
-    for copy in copies:
-        copy.start()
-    for copy in copies:
-        copy.wait()
+def edges_kernel(last, count, adjoint, top, bottom, left, right):
+    step = pl.program_id(0)
+    left[...] = adjoint[:, :, adjoint.shape[2] - BY :]
+    right[...] = adjoint[:, :, :BY]
+
+    @pl.when(step < count)
+    def _():
+        bottom[...] = adjoint[...]
+
+    @pl.when(step >= last)
+    def _():
+        top[...] = adjoint[...]
 
 
 def edges(adjoint):
     parts, shard_z, shard_y, extent = adjoint.shape
-    planes = jax.ShapeDtypeStruct((parts, BAND, shard_y, extent), jnp.float32)
-    lines = jax.ShapeDtypeStruct((parts, shard_z, BY, extent), jnp.float32)
-    hbm = pl.BlockSpec(memory_space=pl.ANY)
-    return pl.pallas_call(
-        edges_kernel,
-        in_specs=[hbm],
-        out_specs=[hbm] * 4,
-        out_shape=[planes, planes, lines, lines],
-        scratch_shapes=[pltpu.SemaphoreType.DMA((4,))],
+    planes = 4
+    count = BAND // planes
+    steps = shard_z // planes
+    last = steps - count
+    plane_shape = jax.ShapeDtypeStruct((parts, BAND, shard_y, extent), jnp.float32)
+    line_shape = jax.ShapeDtypeStruct((parts, shard_z, BY, extent), jnp.float32)
+    block = (parts, planes, shard_y, extent)
+    line = pl.BlockSpec((parts, planes, BY, extent), lambda i: (0, i, 0, 0))
+    return pl.pallas_call(
+        functools.partial(edges_kernel, last, count),
+        grid=(steps,),
+        in_specs=[pl.BlockSpec(block, lambda i: (0, i, 0, 0))],
+        out_specs=[
+            pl.BlockSpec(block, lambda i: (0, jnp.maximum(i - last, 0), 0, 0)),
+            pl.BlockSpec(block, lambda i: (0, jnp.minimum(i, count - 1), 0, 0)),
+            line,
+            line,
+        ],
+        out_shape=[plane_shape, plane_shape, line_shape, line_shape],
         compiler_params=params(),
         cost_estimate=cost(1e6, 4e7),
         name="edges",

time: 784 us -> 227 us (0.29)
  Pallas kernels: 682 us -> 123 us
    pallas_call x1, Pallas kernels: 573 us -> 15.4 us  [edges(): pl.pallas_call(functools.partial(edges_kernel, last, count), grid=(steps,...]
  transfers between devices with their start and end apart: 13 -> 13, of which waited for: 3 -> 3; matrix products, arithmetic and copies ran while one was open for 1% -> 5% of each run, Pallas kernels for 14% -> 48%
where the time goes in v5:
time: 227 us; the launch traced here: 226 us
  Pallas kernels  123 us (54%)
  waiting for transfers between devices  53.7 us (24%)
  starting transfers between devices  35.7 us (16%)
  other arithmetic  8.43 us (4%)
  local copies, waits for them, and re-layouts  4.06 us (2%)
    ppermute x4, waiting for transfers between devices, send_up(): return lax.ppermute(value, axis, [(i, i + 1) for i in range(size - 1)])  42.2 us
    pallas_call x1, Pallas kernels, xy_terms(): pl.pallas_call(xy_kernel, grid=(shard_z // planes,), in_specs=[whole(m) f...  34.4 us
    pallas_call x1, Pallas kernels, z_local(): pl.pallas_call(z_local_kernel, grid=(shard_y // GROUP,), in_specs=[pl.Blo...  24.4 us
    pallas_call x1, Pallas kernels, combine(): pl.pallas_call(combine_kernel, grid=(shard_y // GROUP,), in_specs=[whole(...  18.4 us
    ppermute x4, starting transfers between devices, send_up(): return lax.ppermute(value, axis, [(i, i + 1) for i in range(size - 1)])  18.1 us
    pallas_call x1, Pallas kernels, turbine_terms(): pl.pallas_call(functools.partial(turbine_kernel, count, (shard_z, shard_y...  15.7 us
    pallas_call x1, Pallas kernels, edges(): pl.pallas_call(functools.partial(edges_kernel, last, count), grid=(steps,...  15.4 us
    ppermute x5, starting transfers between devices, exchange(): return lax.ppermute(value, axis, [(i, i ^ distance) for i in range(size)])  12.5 us
  transfers between devices with their start and end apart: 13, of which 3 were waited for; matrix products, arithmetic and copies ran while one was open for 5% of the time, Pallas kernels for 48%

profile of v5, /device:TPU:0, one launch (start us, length us, event | category | flops | bytes accessed | tf_op | source)
XLA Modules:
  0.0 225.8 jit_solution(10069252380632881341)
XLA Ops:
  0.6 15.4 %edges.1 = (f32[3,16,64,256]{3,2,1,0:T(8,128)}, f32[3,16,64,256]{3,2,1,0:T(8,128)}, f32[3,64,32,256]{3,2,1,0:T(8,128)}, f32[3,64,32,256]{3,2,1,0:T(8,128)}) custom-call(f32[3,64,64,256]{3,2,1,0:T(8,128)} %adjoint.7), custom_call_target="tpu_custom_call" | custom-call | flops 20000 | bytes 800000 | tf_op jit(solution)/shard_map/edges/pallas_call | solution.py:419
  16.1 4.9 %collective-permute-start.2 = (f32[3,64,32,256]{3,2,1,0:T(8,128)}, f32[3,64,32,256]{3,2,1,0:T(8,128)}, u32[]{:S(2)}, u32[]{:S(2)}) collective-permute-start(f32[3,64,32,256]{3,2,1,0:T(8,128)} %get-tuple-element.41), channel_id=1, source_target_pairs={{0,1},{1,2},{2,3},{4,5},{5,6},{6,7},{8,9},{9,10},{10,11},{12,13},{... | collective-permute-start | bytes 18874376 | tf_op jit(solution)/shard_map/ppermute | solution.py:438
  21.0 1.3 collective-permute-start.3
  22.3 4.5 %collective-permute-start.5 = (f32[3,16,64,256]{3,2,1,0:T(8,128)}, f32[3,16,64,256]{3,2,1,0:T(8,128)S(1)}, u32[]{:S(2)}, u32[]{:S(2)}) collective-permute-start(f32[3,16,64,256]{3,2,1,0:T(8,128)} %get-tuple-element.54), channel_id=1, source_target_pairs={{0,4},{4,8},{8,12},{12,16},{16,20},{20,24},{24,28},{1,5},{5,9},{9,... | collective-permute-start | bytes 9437192 | tf_op jit(solution)/shard_map/ppermute | solution.py:438
  26.8 1.3 collective-permute-start.6
  28.2 0.5 fusion.2
  28.7 0.5 fusion.3.zs
  29.3 15.7 %turbine_terms.1 = (f32[64,64,256]{2,1,0:T(8,128)}, f32[96,128]{1,0:T(8,128)}, f32[96,128]{1,0:T(8,128)}) custom-call(s32[96]{0:T(128)} %fusion.3.zs, s32[96]{0:T(128)} %get-tuple-element.68.ys, s32[96]{0:T(128)} %get-tuple-element.70.xs, f32[96]{0:T(128)} %thrust.1, f32[3,64,64,256]{3,2,1,0:T(8,128)} %adjoint.7, f32[3,64,64,256]{3,2,1,0:T(8,128)} %adjoint.7, ...), custom_call_target="tpu_custom_call" | custom-call | flops 20000 | bytes 600000 | tf_op jit(solution)/shard_map/turbine_terms/pallas_call | solution.py:172
  45.0 0.9 reduce_sum.37
  45.9 0.9 reduce_sum.36
  47.2 1.6 pad_dynamic-slice_fusion.z
  48.8 0.7 pad_dynamic-slice_fusion.1.y
  49.5 3.6 %matrices.1 = (bf16[256,512]{1,0:T(8,128)(2,1)}, bf16[128,256]{1,0:T(8,128)(2,1)}, bf16[128,128]{1,0:T(8,128)(2,1)}, bf16[64,64]{1,0:T(8,128)(2,1)}, bf16[64,64]...) custom-call(f32[256,256]{1,0:T(8,128)} %x.9, ...), custom_call_target="tpu_custom_call" | custom-call | flops 2000000 | bytes 80000 | tf_op jit(solution)/shard_map/matrices/pallas_call | solution.py:103
  53.2 24.4 %z_local.1.tendency = f32[3,64,64,256]{3,2,1,0:T(8,128)} custom-call(bf16[1024,512]{1,0:T(8,128)(2,1)} %get-tuple-element.39.matrix, f32[3,64,64,256]{3,2,1,0:T(8,128)} %adjoint.7, f32[3,64,64,256]{3,2,1,0:T(8,128)} %carrier.1), custom_call_target="tpu_custom_call" | custom-call | flops 400000000 | bytes 800000 | tf_op jit(solution)/shard_map/z_local/pallas_call | solution.py:224
  77.6 4.7 %collective-permute-start.1 = (f32[2,96]{1,0:T(2,128)S(1)}, f32[2,96]{1,0:T(2,128)S(1)}, u32[]{:S(2)}, u32[]{:S(2)}) collective-permute-start(f32[2,96]{1,0:T(2,128)S(1)} %fusion.4), channel_id=1, source_target_pairs={{0,2},{1,3},{2,0},{3,1},{4,6},{5,7},{6,4},{7,5},{8,10},{9,11},{10,... | collective-permute-start | bytes 2312 | tf_op jit(solution)/shard_map/ppermute | solution.py:448
  82.3 11.5 %collective-permute-done.1 = f32[2,96]{1,0:T(2,128)S(1)} collective-permute-done((f32[2,96]{1,0:T(2,128)S(1)}, f32[2,96]{1,0:T(2,128)S(1)}, u32[]{:S(2)}, u32[]{:S(2)}) %collective-permute-start.1) | collective-permute-done | bytes 800 | tf_op jit(solution)/shard_map/ppermute | solution.py:448
  93.8 34.4 %xy_terms.1 = (f32[3,64,64,256]{3,2,1,0:T(8,128)}, f32[64,32,256]{2,1,0:T(8,128)}, f32[64,32,256]{2,1,0:T(8,128)}) custom-call(bf16[256,512]{1,0:T(8,128)(2,1)} %get-tuple-element.44.matrix_x, bf16[128,256]{1,0:T(8,128)(2,1)} %get-tuple-element.45.matrix_ya, bf16[128,128]{1,0:T(8,128)(2,1)} %get-tuple-element.46.matrix_yv, ...), custom_call_target="tpu_custom_call" | custom-call | flops 400000000 | bytes 1400000 | tf_op jit(solution)/shard_map/xy_terms/pallas_call | solution.py:287
  128.1 1.3 collective-permute-start.11
  129.4 4.4 %collective-permute-start.10 = (f32[64,32,256]{2,1,0:T(8,128)}, f32[64,32,256]{2,1,0:T(8,128)}, u32[]{:S(2)}, u32[]{:S(2)}) collective-permute-start(f32[64,32,256]{2,1,0:T(8,128)} %get-tuple-element.64), channel_id=1, source_target_pairs={{0,1},{1,2},{2,3},{4,5},{5,6},{6,7},{8,9},{9,10},{10,11},{12,13},{... | collective-permute-start | bytes 6291464 | tf_op jit(solution)/shard_map/ppermute | solution.py:438
  133.8 1.6 collective-permute-start.4
  135.4 27.2 %collective-permute-done.5.halo_low = f32[3,16,64,256]{3,2,1,0:T(8,128)S(1)} collective-permute-done((f32[3,16,64,256]{3,2,1,0:T(8,128)}, f32[3,16,64,256]{3,2,1,0:T(8,128)S(1)}, u32[]{:S(2)}, u32[]{:S(2)}) %collective-permute-start.5) | collective-permute-done | bytes 3145760 | tf_op jit(solution)/shard_map/ppermute | solution.py:438
  162.6 1.6 copy-done.2
  164.3 7.1 %z_back.1 = (f32[16,64,256]{2,1,0:T(8,128)S(1)}, f32[16,64,256]{2,1,0:T(8,128)}) custom-call(bf16[256,256]{1,0:T(8,128)(2,1)S(1)} %copy-done, bf16[256,256]{1,0:T(8,128)(2,1)S(1)} %copy-done.1, f32[3,64,64,256]{3,2,1,0:T(8,128)} %carrier.1, f32[3,64,64,256]{3,2,1,0:T(8,128)} %carrier.1, f32[3,16,64,256]{3,2,1,0:T(8,128)} %copy-done.2, ...), custom_call_target="tpu_custom_call" | custom-call | flops 60000000 | bytes 400000 | tf_op jit(solution)/shard_map/z_back/pallas_call | solution.py:323
  171.3 4.3 %collective-permute-start.7 = (f32[16,64,256]{2,1,0:T(8,128)}, f32[16,64,256]{2,1,0:T(8,128)S(1)}, u32[]{:S(2)}, u32[]{:S(2)}) collective-permute-start(f32[16,64,256]{2,1,0:T(8,128)} %get-tuple-element.58), channel_id=1, source_target_pairs={{0,4},{4,8},{8,12},{12,16},{16,20},{20,24},{24,28},{1,5},{5,9},{9,... | collective-permute-start | bytes 3145736 | tf_op jit(solution)/shard_map/ppermute | solution.py:438
  175.7 1.3 collective-permute-start.8
  177.2 3.2 %collective-permute-start.9 = (f32[2,96]{1,0:T(2,128)S(1)}, f32[2,96]{1,0:T(2,128)S(1)}, u32[]{:S(2)}, u32[]{:S(2)}) collective-permute-start(f32[2,96]{1,0:T(2,128)S(1)} %add.55), channel_id=1, source_target_pairs={{0,8},{4,12},{8,0},{12,4},{16,24},{20,28},{24,16},{28,20},{1,9},{5... | collective-permute-start | bytes 2312 | tf_op jit(solution)/shard_map/ppermute | solution.py:448
  180.4 4.7 %pad_add_fusion.stretch_y = f32[64,64,256]{2,1,0:T(8,128)} fusion(f32[64,32,256]{2,1,0:T(8,128)} %collective-permute-done.11, f32[64,32,256]{2,1,0:T(8,128)} %collective-permute-done.10), kind=kLoop, calls=%fused_computation | loop fusion | flops 1048576 | bytes 8388608 | tf_op jit(solution)/shard_map/add | solution.py:506
  185.0 18.4 %combine.1.updated = f32[3,64,64,256]{3,2,1,0:T(8,128)} custom-call(bf16[256,256]{1,0:T(8,128)(2,1)} %get-tuple-element.61.from_low, bf16[256,256]{1,0:T(8,128)(2,1)} %get-tuple-element.62.from_high, f32[3,64,64,256]{3,2,1,0:T(8,128)} %adjoint.7, f32[3,64,64,256]{3,2,1,0:T(8,128)} %carrier.1, f32[3,64,64,256]{3,2,1,0:T(8,128)} %get-tuple-element.63.tendency, ...), custom_call_target="tpu_custom_call" | custom-call | flops 60000000 | bytes 1000000 | tf_op jit(solution)/shard_map/combine/pallas_call | solution.py:359
  203.5 2.7 %collective-permute-start.12 = (f32[2,96]{1,0:T(2,128)S(1)}, f32[2,96]{1,0:T(2,128)S(1)}, u32[]{:S(2)}, u32[]{:S(2)}) collective-permute-start(f32[2,96]{1,0:T(2,128)S(1)} %add.58), channel_id=1, source_target_pairs={{0,16},{4,20},{8,24},{12,28},{16,0},{20,4},{24,8},{28,12},{1,17},{... | collective-permute-start | bytes 2312 | tf_op jit(solution)/shard_map/ppermute | solution.py:448
  206.1 15.0 %collective-permute-done.7.back_low = f32[16,64,256]{2,1,0:T(8,128)S(1)} collective-permute-done((f32[16,64,256]{2,1,0:T(8,128)}, f32[16,64,256]{2,1,0:T(8,128)S(1)}, u32[]{:S(2)}, u32[]{:S(2)}) %collective-permute-start.7) | collective-permute-done | bytes 1048608 | tf_op jit(solution)/shard_map/ppermute | solution.py:438
  221.1 4.0 %finish.1 = f32[3,64,64,256]{3,2,1,0:T(8,128)} custom-call(f32[16,64,256]{2,1,0:T(8,128)S(1)} %collective-permute-done.7.back_low, f32[16,64,256]{2,1,0:T(8,128)S(1)} %collective-permute-done.8.back_high, f32[3,64,64,256]{3,2,1,0:T(8,128)} %combine.1.updated), custom_call_target="tpu_custom_call", output_to_operand_aliasing={{}: (2, {})} | custom-call | flops 20000 | bytes 120000 | tf_op jit(solution)/shard_map/finish/pallas_call | solution.py:382
  225.1 0.7 select_reduce_fusion
  (32 shorter events, 0.7 us)
Async XLA Ops:
  0.6 27.5 %copy-start.4 = (s32[96,128]{1,0:T(8,128)S(1)}, s32[96,128]{1,0:T(8,128)}, u32[]{:S(2)}) copy-start(s32[96,128]{1,0:T(8,128)} %param.14) | copy-start | bytes 147460
  16.1 77.7 %collective-permute-start.2 = (f32[3,64,32,256]{3,2,1,0:T(8,128)}, f32[3,64,32,256]{3,2,1,0:T(8,128)}, u32[]{:S(2)}, u32[]{:S(2)}) collective-permute-start(f32[3,64,32,256]{3,2,1,0:T(8,128)} %get-tuple-element.41), channel_id=1, source_target_pairs={{0,1},{1,2},{2,3},{4,5},{5,6},{6,7},{8,9},{9,10},{10,11},{12,13},{... | collective-permute-start | bytes 18874376 | tf_op jit(solution)/shard_map/ppermute | solution.py:438
  21.0 72.7 %collective-permute-start.3 = (f32[3,64,32,256]{3,2,1,0:T(8,128)}, f32[3,64,32,256]{3,2,1,0:T(8,128)}, u32[]{:S(2)}, u32[]{:S(2)}) collective-permute-start(f32[3,64,32,256]{3,2,1,0:T(8,128)} %get-tuple-element.42), channel_id=1, source_target_pairs={{1,0},{2,1},{3,2},{5,4},{6,5},{7,6},{9,8},{10,9},{11,10},{13,12},{... | collective-permute-start | bytes 18874376 | tf_op jit(solution)/shard_map/ppermute | solution.py:443
  22.3 140.3 %collective-permute-start.5 = (f32[3,16,64,256]{3,2,1,0:T(8,128)}, f32[3,16,64,256]{3,2,1,0:T(8,128)S(1)}, u32[]{:S(2)}, u32[]{:S(2)}) collective-permute-start(f32[3,16,64,256]{3,2,1,0:T(8,128)} %get-tuple-element.54), channel_id=1, source_target_pairs={{0,4},{4,8},{8,12},{12,16},{16,20},{20,24},{24,28},{1,5},{5,9},{9,... | collective-permute-start | bytes 9437192 | tf_op jit(solution)/shard_map/ppermute | solution.py:438
  26.8 135.8 %collective-permute-start.6 = (f32[3,16,64,256]{3,2,1,0:T(8,128)}, f32[3,16,64,256]{3,2,1,0:T(8,128)}, u32[]{:S(2)}, u32[]{:S(2)}) collective-permute-start(f32[3,16,64,256]{3,2,1,0:T(8,128)} %get-tuple-element.55), channel_id=1, source_target_pairs={{4,0},{8,4},{12,8},{16,12},{20,16},{24,20},{28,24},{5,1},{9,5},{13... | collective-permute-start | bytes 9437192 | tf_op jit(solution)/shard_map/ppermute | solution.py:443
  29.3 19.5 %copy-start.3 = (f32[256,256]{1,0:T(8,128)S(1)}, f32[256,256]{1,0:T(8,128)}, u32[]{:S(2)}) copy-start(f32[256,256]{1,0:T(8,128)} %param.12) | copy-start | bytes 786436
  46.9 30.7 %collective-permute-start = (f32[2,96]{1,0:T(2,128)S(1)}, f32[2,96]{1,0:T(2,128)S(1)}, u32[]{:S(2)}, u32[]{:S(2)}) collective-permute-start(f32[2,96]{1,0:T(2,128)S(1)} %maximum_multiply_fusion), channel_id=1, source_target_pairs={{0,1},{1,0},{2,3},{3,2},{4,5},{5,4},{6,7},{7,6},{8,9},{9,8},{10,11... | collective-permute-start | bytes 2312 | tf_op jit(solution)/shard_map/ppermute | solution.py:448
  77.6 16.2 %collective-permute-start.1 = (f32[2,96]{1,0:T(2,128)S(1)}, f32[2,96]{1,0:T(2,128)S(1)}, u32[]{:S(2)}, u32[]{:S(2)}) collective-permute-start(f32[2,96]{1,0:T(2,128)S(1)} %fusion.4), channel_id=1, source_target_pairs={{0,2},{1,3},{2,0},{3,1},{4,6},{5,7},{6,4},{7,5},{8,10},{9,11},{10,... | collective-permute-start | bytes 2312 | tf_op jit(solution)/shard_map/ppermute | solution.py:448
  93.7 70.5 %copy-start = (bf16[256,256]{1,0:T(8,128)(2,1)S(1)}, bf16[256,256]{1,0:T(8,128)(2,1)}, u32[]{:S(2)}) copy-start(bf16[256,256]{1,0:T(8,128)(2,1)} %get-tuple-element.35.edge_low) | copy-start | bytes 393220
  93.8 70.5 %copy-start.1 = (bf16[256,256]{1,0:T(8,128)(2,1)S(1)}, bf16[256,256]{1,0:T(8,128)(2,1)}, u32[]{:S(2)}) copy-start(bf16[256,256]{1,0:T(8,128)(2,1)} %get-tuple-element.36.edge_high) | copy-start | bytes 393220
  128.1 52.2 %collective-permute-start.11 = (f32[64,32,256]{2,1,0:T(8,128)}, f32[64,32,256]{2,1,0:T(8,128)}, u32[]{:S(2)}, u32[]{:S(2)}) collective-permute-start(f32[64,32,256]{2,1,0:T(8,128)} %get-tuple-element.65), channel_id=1, source_target_pairs={{1,0},{2,1},{3,2},{5,4},{6,5},{7,6},{9,8},{10,9},{11,10},{13,12},{... | collective-permute-start | bytes 6291464 | tf_op jit(solution)/shard_map/ppermute | solution.py:443
  129.4 50.9 %collective-permute-start.10 = (f32[64,32,256]{2,1,0:T(8,128)}, f32[64,32,256]{2,1,0:T(8,128)}, u32[]{:S(2)}, u32[]{:S(2)}) collective-permute-start(f32[64,32,256]{2,1,0:T(8,128)} %get-tuple-element.64), channel_id=1, source_target_pairs={{0,1},{1,2},{2,3},{4,5},{5,6},{6,7},{8,9},{9,10},{10,11},{12,13},{... | collective-permute-start | bytes 6291464 | tf_op jit(solution)/shard_map/ppermute | solution.py:438
  133.8 28.8 %collective-permute-start.4 = (f32[2,96]{1,0:T(2,128)S(1)}, f32[2,96]{1,0:T(2,128)S(1)}, u32[]{:S(2)}, u32[]{:S(2)}) collective-permute-start(f32[2,96]{1,0:T(2,128)S(1)} %fusion.5), channel_id=1, source_target_pairs={{0,4},{4,0},{8,12},{12,8},{16,20},{20,16},{24,28},{28,24},{1,5},{5... | collective-permute-start | bytes 2312 | tf_op jit(solution)/shard_map/ppermute | solution.py:448
  162.6 1.6 copy-start.2
  164.3 12.7 %copy-start.5 = (s32[96]{0:T(128)S(1)}, s32[96]{0:T(128)}, u32[]{:S(2)}) copy-start(s32[96]{0:T(128)} %param.15) | copy-start | bytes 1156
  171.3 49.8 %collective-permute-start.7 = (f32[16,64,256]{2,1,0:T(8,128)}, f32[16,64,256]{2,1,0:T(8,128)S(1)}, u32[]{:S(2)}, u32[]{:S(2)}) collective-permute-start(f32[16,64,256]{2,1,0:T(8,128)} %get-tuple-element.58), channel_id=1, source_target_pairs={{0,4},{4,8},{8,12},{12,16},{16,20},{20,24},{24,28},{1,5},{5,9},{9,... | collective-permute-start | bytes 3145736 | tf_op jit(solution)/shard_map/ppermute | solution.py:438
  175.7 45.4 %collective-permute-start.8 = (f32[16,64,256]{2,1,0:T(8,128)S(1)}, f32[16,64,256]{2,1,0:T(8,128)S(1)}, u32[]{:S(2)}, u32[]{:S(2)}) collective-permute-start(f32[16,64,256]{2,1,0:T(8,128)S(1)} %get-tuple-element.59), channel_id=1, source_target_pairs={{4,0},{8,4},{12,8},{16,12},{20,16},{24,20},{28,24},{5,1},{9,5},{13... | collective-permute-start | bytes 3145736 | tf_op jit(solution)/shard_map/ppermute | solution.py:443
  177.2 26.3 %collective-permute-start.9 = (f32[2,96]{1,0:T(2,128)S(1)}, f32[2,96]{1,0:T(2,128)S(1)}, u32[]{:S(2)}, u32[]{:S(2)}) collective-permute-start(f32[2,96]{1,0:T(2,128)S(1)} %add.55), channel_id=1, source_target_pairs={{0,8},{4,12},{8,0},{12,4},{16,24},{20,28},{24,16},{28,20},{1,9},{5... | collective-permute-start | bytes 2312 | tf_op jit(solution)/shard_map/ppermute | solution.py:448
  203.5 21.6 %collective-permute-start.12 = (f32[2,96]{1,0:T(2,128)S(1)}, f32[2,96]{1,0:T(2,128)S(1)}, u32[]{:S(2)}, u32[]{:S(2)}) collective-permute-start(f32[2,96]{1,0:T(2,128)S(1)} %add.58), channel_id=1, source_target_pairs={{0,16},{4,20},{8,24},{12,28},{16,0},{20,4},{24,8},{28,12},{1,17},{... | collective-permute-start | bytes 2312 | tf_op jit(solution)/shard_map/ppermute | solution.py:448
